TPU v7x, 256 devices: a whole 4x4x8 slice. The times are simulated.
256 devices in a mesh: px: 8 (over z), py: 32 (over x, y, core).
Axes of the slice: x: 4, y: 4, z: 8, core: 2. Of those that a mesh axis runs over, the one named last changes fastest.
Arguments:
- right_side: float32 [8, 2048, 2048], P(None, 'py', 'px'), may hold values from -6 to 6
- solution_in: float32 [8, 2048, 2048], P(None, 'py', 'px'), may hold values from -4 to 4
- classes: int32 [8, 2048, 2048], P(None, 'py', 'px'), may hold values from 0 to 15
- coeff_table: float32 [16], replicated, may hold values from 0.2 to 5
- eigenvectors: bfloat16 [2048, 2048], replicated, may hold values from -0.053880558 to 0.053880558, as said below
- eigenvalues: float32 [2048], replicated, may hold values from 0.01 to 4
- level_shift: float32 [8], replicated, may hold values from 0.3 to 3
Outputs:
- solution: float32 [8, 2048, 2048], P(None, 'py', 'px')
- residual: float32 [8, 2048, 2048], P(None, 'py', 'px')
- direction: float32 [8, 2048, 2048], P(None, 'py', 'px')
Inputs may be any that keep to these rules, and one draw needn't show every extreme that they name: eigenvectors is a symmetric matrix.
All inputs are finite; a program needn't handle non-finite values.
Results may differ from a plain program's by a relative error of at most 0.034.
Values may be sent and summed in bfloat16 or wider, within the bound.
A program may use at most 64 MiB of HBM per device.

v0:
```python
import jax
import jax.numpy as jnp
from jax import lax
from jax.sharding import PartitionSpec as P

ITERS = 2


def padded_2(array, sides, width):
    for axis, dim in sides:
        size, length = (lax.axis_size(axis), array.shape[dim])
        up = [(i, (i + 1) % size) for i in range(size - 1)]
        down = [(j, i) for i, j in up]
        last = lax.slice_in_dim(array, length - width, length, axis=dim)
        initial = lax.slice_in_dim(array, 0, width, axis=dim)
        before = lax.ppermute(last, axis, up)
        after = lax.ppermute(initial, axis, down)
        array = jnp.concatenate([before, array, after], axis=dim)
    return array


def for_sending(array):

    def short(part):
        return part.astype(jnp.bfloat16) if part.dtype == jnp.float32 else part

    return jax.tree.map(short, array)


def face_sum(padded, coeff_pad):
    values = padded[:, 1:-1, 1:-1]
    coeff = coeff_pad[:, 1:-1, 1:-1]
    height = values.shape[1]
    width = values.shape[2]
    result = jnp.zeros_like(values)
    for shift_y, shift_x in ((0, 1), (2, 1), (1, 0), (1, 2)):
        neighbour = padded[:, shift_y : shift_y + height, shift_x : shift_x + width]
        other = coeff_pad[:, shift_y : shift_y + height, shift_x : shift_x + width]
        result = result + 0.5 * (coeff + other) * (values - neighbour)
    vertical = 0.5 * (coeff[:-1] + coeff[1:]) * (values[:-1] - values[1:])
    zero_layer = jnp.zeros_like(values[:1])
    result = (
        result
        + jnp.concatenate((vertical, zero_layer), 0)
        - jnp.concatenate((zero_layer, vertical), 0)
    )
    return result


def precondition(residual, eigenvectors, eigenvalues, level_shift):
    rounded = residual.astype(jnp.bfloat16)
    levels_here = residual.shape[0] // lax.axis_size("px")
    first = jnp.einsum(
        "kyx,xi->kyi",
        lax.all_to_all(rounded, "px", split_axis=0, concat_axis=2, tiled=True),
        eigenvectors,
        preferred_element_type=jnp.float32,
    ).astype(jnp.bfloat16)
    second = jnp.einsum(
        "kyi,yj->kji",
        lax.all_to_all(first, "py", split_axis=2, concat_axis=1, tiled=True),
        eigenvectors,
        preferred_element_type=jnp.float32,
    )
    spectral_cols = second.shape[2]
    eigen_cols = lax.dynamic_slice_in_dim(
        eigenvalues, lax.axis_index("py") * spectral_cols, spectral_cols, 0
    )
    shift_here = lax.dynamic_slice_in_dim(
        level_shift, lax.axis_index("px") * levels_here, levels_here, 0
    )
    denom = eigenvalues[None, :, None] + eigen_cols[None, None, :] + shift_here[:, None, None]
    scaled = (second / denom).astype(jnp.bfloat16)
    fourth = jnp.einsum(
        "kji,yj->kyi", scaled, eigenvectors, preferred_element_type=jnp.float32
    ).astype(jnp.bfloat16)
    returned = lax.all_to_all(fourth, "py", split_axis=1, concat_axis=2, tiled=True)
    pencil = jnp.einsum("kyi,xi->kyx", returned, eigenvectors, preferred_element_type=jnp.float32)
    return lax.all_to_all(
        pencil.astype(jnp.bfloat16), "px", split_axis=2, concat_axis=0, tiled=True
    ).astype(pencil.dtype)


def shards(right_side, solution_in, classes, coeff_table, eigenvectors, eigenvalues, level_shift):
    coeff = jnp.zeros(classes.shape, jnp.float32)
    for label in range(coeff_table.shape[0]):
        coeff = jnp.where(classes == label, coeff_table[label], coeff)
    stacked = padded_2(
        jnp.stack((solution_in, coeff)).astype(jnp.bfloat16), (("px", 3), ("py", 2)), 1
    ).astype(jnp.float32)
    coeff_pad = stacked[1]
    solution = solution_in
    residual = right_side - face_sum(stacked[0], coeff_pad)
    direction = jnp.zeros_like(residual)
    gamma_prev = jnp.float32(1.0)
    for iteration in range(ITERS):
        precond = precondition(residual, eigenvectors, eigenvalues, level_shift)
        gamma = lax.psum(jnp.sum(residual * precond), ("px", "py"))
        if iteration == 0:
            direction = precond
        else:
            direction = precond + gamma / gamma_prev * direction
        padded = padded_2(for_sending(direction), (("px", 2), ("py", 1)), 1).astype(direction.dtype)
        image = face_sum(padded, coeff_pad)
        alpha = gamma / lax.psum(jnp.sum(direction * image), ("px", "py"))
        solution = solution + alpha * direction
        residual = residual - alpha * image
        gamma_prev = gamma
    return (solution, residual, direction)


def solution(mesh):
    in_specs = (P(None, "py", "px"), P(None, "py", "px"), P(None, "py", "px"), P(), P(), P(), P())
    out_specs = (P(None, "py", "px"), P(None, "py", "px"), P(None, "py", "px"))
    return jax.shard_map(shards, mesh=mesh, in_specs=in_specs, out_specs=out_specs, check_vma=False)
```

profile of v0, /device:TPU:1, one launch (start us, length us, event | category | flops | bytes accessed | tf_op | source)
XLA Modules:
  0.0 568.3 jit_solution(7523217841468684797)
XLA Ops:
  2.6 12.1 %fusion.53 = (bf16[1,8,64,256]{3,1,2,0:T(8,128)(2,1)S(1)}, bf16[1,8,64,256]{3,1,2,0:T(8,128)(2,1)S(1)}) fusion(f32[8,64,256]{2,1,0:T(8,128)} %param.8, bf16[]{:T(256)} %bitcast.16, bf16[]{:T(256)} %bitcast.15, bf16[]{:T(256)} %bitcast.14, bf16[]{:T(256)} %bitcast.13, bf16[]{:T(256)} %bitcast.12, bf16[]{:T(256)} %bitcast.11, bf16[]{:T(256)} %bitcast.10, ...), kind=kLoop, calls=%fused_computation.99 | loop fusion | flops 4194304 | bytes 1572896 | tf_op jit(solution)/shard_map/stack | solution.py:89
  14.8 4.4 collective-permute-start
  20.5 3.6 collective-permute-done
  24.2 4.2 collective-permute-done.1
  28.4 4.8 collective-permute-start.2
  40.9 18.6 %all_to_all.117 = bf16[8,64,256]{2,1,0:T(8,128)(2,1)S(1)} all-to-all(bf16[8,64,256]{2,1,0:T(8,128)(2,1)S(1)} %copy.132), channel_id=1, replica_groups=mesh['px'=8,'py'=32] {'px'}, dimensions={0} | all-to-all | bytes 524288 | tf_op jit(solution)/shard_map/all_to_all | solution.py:55
  62.5 11.5 %reduce = bf16[2048,64]{1,0:T(8,128)(2,1)S(1)} reduce(bf16[2048,1,64]{2,1,0:T(2,128)(2,1)S(1)} %bitcast.188, bf16[]{:T(256)} %broadcast.67), dimensions={1}, to_apply=%bitcast.140.reduce_sub_computation | reduce | bytes 524290
  75.1 8.8 %all-to-all-start.1 = ((bf16[32,2,2048]{2,1,0:T(2,128)(2,1)}), bf16[32,2,2048]{2,1,0:T(2,128)(2,1)S(1)}, u32[]{:S(2)}, u32[]{:S(2)}) async-start(bf16[32,2,2048]{2,1,0:T(2,128)(2,1)} %reshape.79), calls=%async_computation.1 | async-start | bytes 524288 | tf_op jit(solution)/shard_map/all_to_all | solution.py:61
  84.7 8.2 %all-to-all-done.1 = bf16[32,2,2048]{2,1,0:T(2,128)(2,1)S(1)} async-done(((bf16[32,2,2048]{2,1,0:T(2,128)(2,1)}), bf16[32,2,2048]{2,1,0:T(2,128)(2,1)S(1)}, u32[]{:S(2)}, u32[]{:S(2)}) %all-to-all-start.1) | async-done | bytes 262176 | tf_op jit(solution)/shard_map/all_to_all | solution.py:61
  96.2 10.6 %fusion.5 = bf16[1,2048,64]{1,2,0:T(8,128)(2,1)S(1)} fusion(bf16[2048,2048]{1,0:T(8,128)(2,1)} %param.11, bf16[2048,64]{0,1:T(8,128)(2,1)S(1)} %reshape.72, f32[]{:T(128)} %bitcast.25, f32[64]{0:T(128)S(1)} %dynamic_slice.8, f32[2048]{0:T(1024)S(1)} %copy-done.2), kind=kOutput, calls=%fused_computation.13 | convolution fusion | flops 1074397184 | bytes 8921348 | tf_op jit(solution)/shard_map/kji,yj->kyi/dot_general | solution.py:74
  107.5 11.5 %reduce.1 = bf16[2048,64]{1,0:T(8,128)(2,1)S(1)} reduce(bf16[2048,1,64]{2,1,0:T(2,128)(2,1)S(1)} %bitcast.190, bf16[]{:T(256)} %broadcast.67), dimensions={1}, to_apply=%bitcast.142.reduce_sub_computation | reduce | bytes 524290
  119.4 12.7 %all_to_all.118 = bf16[32,2,2048]{2,1,0:T(2,128)(2,1)S(1)} all-to-all(bf16[32,2,2048]{2,1,0:T(2,128)(2,1)S(1)} %reshape.81), channel_id=1, replica_groups=mesh['px'=8,'py'=32] {'py'}, dimensions={0} | all-to-all | bytes 524288 | tf_op jit(solution)/shard_map/all_to_all | solution.py:77
  135.4 6.0 %fusion.6 = bf16[1,64,2048]{2,1,0:T(8,128)(2,1)S(1)} fusion(bf16[64,2048]{1,0:T(8,128)(2,1)S(1)} %reshape.73, bf16[2048,2048]{1,0:T(8,128)(2,1)} %param.11), kind=kOutput, calls=%fused_computation.14 | convolution fusion | flops 537001984 | bytes 8912896 | tf_op jit(solution)/shard_map/kyi,xi->kyx/dot_general | solution.py:78
  142.2 11.5 %reduce.2 = bf16[2048,64]{1,0:T(8,128)(2,1)S(1)} reduce(bf16[2048,1,64]{2,1,0:T(2,128)(2,1)S(1)} %bitcast.191, bf16[]{:T(256)} %broadcast.67), dimensions={1}, to_apply=%bitcast.144.reduce_sub_computation | reduce | bytes 524290
  154.1 14.8 %all_to_all.119 = bf16[8,2,8192]{2,1,0:T(2,128)(2,1)S(1)} all-to-all(bf16[8,2,8192]{2,1,0:T(2,128)(2,1)S(1)} %reshape.83), channel_id=1, replica_groups=mesh['px'=8,'py'=32] {'px'}, dimensions={0} | all-to-all | bytes 524288 | tf_op jit(solution)/shard_map/all_to_all | solution.py:79
  173.6 3.8 collective-permute-done.5
  177.4 4.8 collective-permute-start.6
  189.9 75.7 %all-reduce.6 = (f32[]{:T(128)}, f32[]{:T(128)}) all-reduce(f32[]{:T(128)} %get-tuple-element.13, f32[]{:T(128)} %get-tuple-element.12), channel_id=1, replica_groups=mesh['px'=8,'py'=32] {'px','py'}, use_global_device_ids=true, to_apply=%region_1.2 | all-reduce | flops 2 | bytes 16 | tf_op jit(solution)/shard_map/psum | solution.py:98
  267.0 14.4 %all_to_all.120 = bf16[8,64,256]{2,1,0:T(8,128)(2,1)S(1)} all-to-all(bf16[8,64,256]{2,1,0:T(8,128)(2,1)S(1)} %copy.143), channel_id=1, replica_groups=mesh['px'=8,'py'=32] {'px'}, dimensions={0} | all-to-all | bytes 524288 | tf_op jit(solution)/shard_map/all_to_all | solution.py:55
  281.4 5.0 fusion.7
  287.2 11.5 %reduce.3 = bf16[2048,64]{1,0:T(8,128)(2,1)S(1)} reduce(bf16[2048,1,64]{2,1,0:T(2,128)(2,1)S(1)} %bitcast.192, bf16[]{:T(256)} %broadcast.67), dimensions={1}, to_apply=%bitcast.146.reduce_sub_computation | reduce | bytes 524290
  299.1 15.7 %all_to_all.121 = bf16[32,2,2048]{2,1,0:T(2,128)(2,1)S(1)} all-to-all(bf16[32,2,2048]{2,1,0:T(2,128)(2,1)S(1)} %reshape.85), channel_id=1, replica_groups=mesh['px'=8,'py'=32] {'py'}, dimensions={0} | all-to-all | bytes 524288 | tf_op jit(solution)/shard_map/all_to_all | solution.py:61
  318.1 10.6 %fusion.8 = bf16[1,2048,64]{1,2,0:T(8,128)(2,1)S(1)} fusion(bf16[2048,2048]{1,0:T(8,128)(2,1)} %param.11, bf16[2048,64]{0,1:T(8,128)(2,1)S(1)} %reshape.75, f32[]{:T(128)} %bitcast.25, f32[64]{0:T(128)S(1)} %dynamic_slice.8, f32[2048]{0:T(1024)S(1)} %copy-done.2), kind=kOutput, calls=%fused_computation.16 | convolution fusion | flops 1074397184 | bytes 8921348 | tf_op jit(solution)/shard_map/kji,yj->kyi/dot_general | solution.py:74
  329.4 11.5 %reduce.4 = bf16[2048,64]{1,0:T(8,128)(2,1)S(1)} reduce(bf16[2048,1,64]{2,1,0:T(2,128)(2,1)S(1)} %bitcast.193, bf16[]{:T(256)} %broadcast.67), dimensions={1}, to_apply=%bitcast.148.reduce_sub_computation | reduce | bytes 524290
  341.3 12.7 %all_to_all.122 = bf16[32,2,2048]{2,1,0:T(2,128)(2,1)S(1)} all-to-all(bf16[32,2,2048]{2,1,0:T(2,128)(2,1)S(1)} %reshape.87), channel_id=1, replica_groups=mesh['px'=8,'py'=32] {'py'}, dimensions={0} | all-to-all | bytes 524288 | tf_op jit(solution)/shard_map/all_to_all | solution.py:77
  357.3 6.0 %fusion.9 = bf16[1,64,2048]{2,1,0:T(8,128)(2,1)S(1)} fusion(bf16[64,2048]{1,0:T(8,128)(2,1)S(1)} %reshape.76, bf16[2048,2048]{1,0:T(8,128)(2,1)} %param.11), kind=kOutput, calls=%fused_computation.17 | convolution fusion | flops 537001984 | bytes 8912896 | tf_op jit(solution)/shard_map/kyi,xi->kyx/dot_general | solution.py:78
  364.1 11.5 %reduce.5 = bf16[2048,64]{1,0:T(8,128)(2,1)S(1)} reduce(bf16[2048,1,64]{2,1,0:T(2,128)(2,1)S(1)} %bitcast.189, bf16[]{:T(256)} %broadcast.67), dimensions={1}, to_apply=%bitcast.150.reduce_sub_computation | reduce | bytes 524290
  376.1 14.8 %all_to_all.123 = bf16[8,2,8192]{2,1,0:T(2,128)(2,1)S(1)} all-to-all(bf16[8,2,8192]{2,1,0:T(2,128)(2,1)S(1)} %reshape.89), channel_id=1, replica_groups=mesh['px'=8,'py'=32] {'px'}, dimensions={0} | all-to-all | bytes 524288 | tf_op jit(solution)/shard_map/all_to_all | solution.py:79
  392.9 73.0 %psum.30 = f32[]{:T(128)} all-reduce(f32[]{:T(128)} %fusion.16), channel_id=1, replica_groups=mesh['px'=8,'py'=32] {'px','py'}, use_global_device_ids=true, to_apply=%region_5.6 | all-reduce | flops 1 | bytes 8 | tf_op jit(solution)/shard_map/psum | solution.py:98
  467.3 3.7 collective-permute-start.8
  476.8 4.0 collective-permute-start.10
  488.4 75.8 %psum.31 = f32[]{:T(128)} all-reduce(f32[]{:T(128)} %get-tuple-element.16), channel_id=1, replica_groups=mesh['px'=8,'py'=32] {'px','py'}, use_global_device_ids=true, to_apply=%region_7.8 | all-reduce | flops 1 | bytes 8 | tf_op jit(solution)/shard_map/psum | solution.py:105
  (101 shorter events, 64.9 us)
Async XLA Ops:
  0.6 39.0 %copy-start.1 = (f32[8,64,256]{2,1,0:T(8,128)S(1)}, f32[8,64,256]{2,1,0:T(8,128)}, u32[]{:S(2)}) copy-start(f32[8,64,256]{2,1,0:T(8,128)} %param.7) | copy-start | bytes 1572868
  14.8 9.3 %collective-permute-start = (bf16[2,8,64,1]{3,1,2,0:T(8,128)(2,1)S(1)}, bf16[2,8,64,1]{3,1,2,0:T(8,128)(2,1)S(1)}, u32[]{:S(2)}, u32[]{:S(2)}) collective-permute-start(bf16[2,8,64,1]{3,1,2,0:T(8,128)(2,1)S(1)} %get-tuple-element.33), channel_id=1, source_target_pairs={{0,32},{32,64},{64,96},{96,128},{128,160},{160,192},{192,224},{1,3... | collective-permute-start | bytes 6152 | tf_op jit(solution)/shard_map/ppermute | solution.py:16
  19.2 9.1 %collective-permute-start.1 = (bf16[2,8,64,1]{3,1,2,0:T(8,128)(2,1)S(1)}, bf16[2,8,64,1]{3,1,2,0:T(8,128)(2,1)S(1)}, u32[]{:S(2)}, u32[]{:S(2)}) collective-permute-start(bf16[2,8,64,1]{3,1,2,0:T(8,128)(2,1)S(1)} %get-tuple-element.34), channel_id=1, source_target_pairs={{32,0},{64,32},{96,64},{128,96},{160,128},{192,160},{224,192},{33,... | collective-permute-start | bytes 6152 | tf_op jit(solution)/shard_map/ppermute | solution.py:17
  28.4 7.0 %collective-permute-start.2 = (bf16[2,8,1,258]{3,1,2,0:T(8,128)(2,1)S(1)}, bf16[2,8,1,258]{3,1,2,0:T(8,128)(2,1)S(1)}, u32[]{:S(2)}, u32[]{:S(2)}) collective-permute-start(bf16[2,8,1,258]{3,1,2,0:T(8,128)(2,1)S(1)} %get-tuple-element.27), channel_id=1, source_target_pairs={{0,1},{1,2},{2,3},{3,4},{4,5},{5,6},{6,7},{7,8},{8,9},{9,10},{10,1... | collective-permute-start | bytes 24776 | tf_op jit(solution)/shard_map/ppermute | solution.py:16
  33.2 26.4 %slice-start = ((s8[8388608]{0:T(1024)(128)(4,1)}), s8[4194304]{0:T(1024)(128)(4,1)S(1)}, s32[]{:S(2)}) async-start(s8[8388608]{0:T(1024)(128)(4,1)} %bitcast.174), calls=%async_computation.8 | async-start | bytes 8388608
  33.2 5.3 collective-permute-start.3
  39.7 19.9 %slice-start.1 = ((s8[8388608]{0:T(1024)(128)(4,1)}), s8[4194304]{0:T(1024)(128)(4,1)S(1)}, s32[]{:S(2)}) async-start(s8[8388608]{0:T(1024)(128)(4,1)} %bitcast.174), calls=%async_computation.9 | async-start | bytes 8388608
  59.6 24.4 %copy-start.2 = (f32[2048]{0:T(1024)S(1)}, f32[2048]{0:T(1024)}, u32[]{:S(2)}) copy-start(f32[2048]{0:T(1024)} %param.12) | copy-start | bytes 24580
  59.6 24.5 %copy-start.3 = (f32[8]{0:T(128)S(1)}, f32[8]{0:T(128)}, u32[]{:S(2)}) copy-start(f32[8]{0:T(128)} %param.13) | copy-start | bytes 100
  75.1 17.7 %all-to-all-start.1 = ((bf16[32,2,2048]{2,1,0:T(2,128)(2,1)}), bf16[32,2,2048]{2,1,0:T(2,128)(2,1)S(1)}, u32[]{:S(2)}, u32[]{:S(2)}) async-start(bf16[32,2,2048]{2,1,0:T(2,128)(2,1)} %reshape.79), calls=%async_computation.1 | async-start | bytes 524288 | tf_op jit(solution)/shard_map/all_to_all | solution.py:61
  170.3 3.2 collective-permute-start.4
  171.6 5.7 %collective-permute-start.5 = (bf16[8,64,1]{2,0,1:T(8,128)(2,1)S(1)}, bf16[8,64,1]{2,0,1:T(8,128)(2,1)S(1)}, u32[]{:S(2)}, u32[]{:S(2)}) collective-permute-start(bf16[8,64,1]{2,0,1:T(8,128)(2,1)S(1)} %get-tuple-element.38), channel_id=1, source_target_pairs={{32,0},{64,32},{96,64},{128,96},{160,128},{192,160},{224,192},{33,... | collective-permute-start | bytes 3080 | tf_op jit(solution)/shard_map/ppermute | solution.py:17
  177.4 7.1 %collective-permute-start.6 = (bf16[8,1,258]{2,0,1:T(8,128)(2,1)S(1)}, bf16[8,1,258]{2,0,1:T(8,128)(2,1)S(1)}, u32[]{:S(2)}, u32[]{:S(2)}) collective-permute-start(bf16[8,1,258]{2,0,1:T(8,128)(2,1)S(1)} %get-tuple-element.31), channel_id=1, source_target_pairs={{0,1},{1,2},{2,3},{3,4},{4,5},{5,6},{6,7},{7,8},{8,9},{9,10},{10,1... | collective-permute-start | bytes 12392 | tf_op jit(solution)/shard_map/ppermute | solution.py:16
  182.2 4.9 collective-permute-start.7
  467.1 99.5 %copy-start = (f32[8,64,256]{2,1,0:T(8,128)S(1)}, f32[8,64,256]{2,1,0:T(8,128)}, u32[]{:S(2)}) copy-start(f32[8,64,256]{2,1,0:T(8,128)} %param.8) | copy-start | bytes 1572868
  467.3 5.9 %collective-permute-start.8 = (bf16[8,64,1]{2,0,1:T(8,128)(2,1)S(1)}, bf16[8,64,1]{2,0,1:T(8,128)(2,1)S(1)}, u32[]{:S(2)}, u32[]{:S(2)}) collective-permute-start(bf16[8,64,1]{2,0,1:T(8,128)(2,1)S(1)} %get-tuple-element.35), channel_id=1, source_target_pairs={{0,32},{32,64},{64,96},{96,128},{128,160},{160,192},{192,224},{1,3... | collective-permute-start | bytes 3080 | tf_op jit(solution)/shard_map/ppermute | solution.py:16
  471.0 5.7 %collective-permute-start.9 = (bf16[8,64,1]{2,0,1:T(8,128)(2,1)S(1)}, bf16[8,64,1]{2,0,1:T(8,128)(2,1)S(1)}, u32[]{:S(2)}, u32[]{:S(2)}) collective-permute-start(bf16[8,64,1]{2,0,1:T(8,128)(2,1)S(1)} %get-tuple-element.36), channel_id=1, source_target_pairs={{32,0},{64,32},{96,64},{128,96},{160,128},{192,160},{224,192},{33,... | collective-permute-start | bytes 3080 | tf_op jit(solution)/shard_map/ppermute | solution.py:17
  476.8 7.2 %collective-permute-start.10 = (bf16[8,1,258]{2,0,1:T(8,128)(2,1)S(1)}, bf16[8,1,258]{2,0,1:T(8,128)(2,1)S(1)}, u32[]{:S(2)}, u32[]{:S(2)}) collective-permute-start(bf16[8,1,258]{2,0,1:T(8,128)(2,1)S(1)} %get-tuple-element.29), channel_id=1, source_target_pairs={{0,1},{1,2},{2,3},{3,4},{4,5},{5,6},{6,7},{7,8},{8,9},{9,10},{10,1... | collective-permute-start | bytes 12392 | tf_op jit(solution)/shard_map/ppermute | solution.py:16
  480.8 4.9 collective-permute-start.11
where the time goes:
time: 578 us; the launch traced here: 568 us
  blocking collectives  328 us (57%)
  other arithmetic  90.5 us (16%)
  starting transfers between devices  42.3 us (7%)
  matrix products  39.7 us (7%)
  waiting for transfers between devices  32.3 us (6%)
  local copies, waits for them, and re-layouts  29.7 us (5%)
    psum x2, blocking collectives, shards(): gamma = lax.psum(jnp.sum(residual * precond), ('px', 'py'))  149 us
    psum x1, blocking collectives, shards(): alpha = gamma / lax.psum(jnp.sum(direction * image), ('px', 'py'))  75.8 us
    unnamed x7, other arithmetic  69.2 us
    all_to_all x2, blocking collectives, precondition(): lax.all_to_all(rounded, 'px', split_axis=0, concat_axis=2, tiled=True)  33 us
    all_to_all x2, blocking collectives, precondition(): lax.all_to_all(pencil.astype(jnp.bfloat16), 'px', split_axis=2, concat_ax...  29.5 us
    all_to_all x2, blocking collectives, precondition(): lax.all_to_all(fourth, 'py', split_axis=1, concat_axis=2, tiled=True)  25.4 us
    ppermute x6, starting transfers between devices, padded_2(): before = lax.ppermute(last, axis, up)  22.9 us
    dot_general x2, matrix products, precondition(): jnp.einsum('kji,yj->kyi', scaled, eigenvectors, preferred_element_type=jn...  21.1 us
  transfers between devices with their start and end apart: 13, of which 10 were waited for; matrix products, arithmetic and copies ran while one was open for 0% of the time, Pallas kernels for 0%

commit v1 on v0

v1 whole, which is shorter than its diff:
```python
import functools

import jax
import jax.numpy as jnp
from jax import lax
from jax.experimental import pallas as pl
from jax.experimental.pallas import tpu as pltpu
from jax.sharding import PartitionSpec as P

F32 = jnp.float32
BF16 = jnp.bfloat16
ROWS = 64
HIGH = lax.Precision.HIGHEST
NT = (((1,), (1,)), ((), ()))
TN = (((0,), (0,)), ((), ()))


def kernel(
    PX,
    PY,
    b_hbm,
    x_hbm,
    cls_hbm,
    table,
    vec_hbm,
    eig,
    shift,
    sol_hbm,
    res_hbm,
    dir_hbm,
    vec,
    cls,
    sol,
    res,
    direction,
    vp_x,
    vp_0,
    vp_1,
    cp,
    halo,
    chalo,
    w_e,
    w_w,
    w_s,
    w_n,
    w_z,
    w_sum,
    image,
    xsend,
    xrecv,
    ysend,
    yrecv,
    zsend,
    zrecv,
    bsend,
    brecv,
    lhs,
    s2,
    s3,
    dinv,
    eigc,
    rsend,
    rrecv,
    csend,
    crecv,
    arx_send,
    arx,
    ary_send,
    ary,
    load_sem,
    store_sem,
    halo_send,
    halo_recv,
    a2a_send,
    a2a_recv,
    ar_send,
    ar_recv,
):
    NZ, XL, N = PX, image.shape[2], vec.shape[0]
    G = N // 256
    p, q = lax.axis_index("px"), lax.axis_index("py")

    def lane(shape):
        return lax.broadcasted_iota(jnp.int32, shape, len(shape) - 1)

    def row(shape):
        return lax.broadcasted_iota(jnp.int32, shape, len(shape) - 2)

    load_cls = pltpu.make_async_copy(cls_hbm, cls, load_sem.at[0])
    load_x = pltpu.make_async_copy(x_hbm, vp_x.at[:, 8 : 8 + ROWS, :], load_sem.at[1])
    load_b = pltpu.make_async_copy(b_hbm, res, load_sem.at[2])
    load_v = pltpu.make_async_copy(vec_hbm, vec, load_sem.at[3])
    load_cls.start()
    load_x.start()
    load_b.start()
    load_v.start()

    barrier = pltpu.get_barrier_semaphore()

    @pl.loop(1, PX)
    def _(t):
        pl.semaphore_signal(barrier, inc=1, device_id={"px": lax.rem(p + t, PX)})

    @pl.loop(1, PY)
    def _(t):
        pl.semaphore_signal(barrier, inc=1, device_id={"py": lax.rem(q + t, PY)})

    load_cls.wait()
    load_x.wait()
    pl.semaphore_wait(barrier, PX - 1 + PY - 1)

    def remote(src, dst, send, recv, where):
        return pltpu.make_async_remote_copy(
            src_ref=src, dst_ref=dst, send_sem=send, recv_sem=recv, device_id=where
        )

    def halo_copies(h):
        up = {"py": lax.rem(q + 1, PY)}
        down = {"py": lax.rem(q + PY - 1, PY)}
        right = {"px": lax.rem(p + 1, PX)}
        left = {"px": lax.rem(p + PX - 1, PX)}
        return [
            remote(rsend.at[h, 0], rrecv.at[h, 1], halo_send.at[h, 0], halo_recv.at[h, 0], down),
            remote(rsend.at[h, 1], rrecv.at[h, 0], halo_send.at[h, 1], halo_recv.at[h, 1], up),
            remote(csend.at[h], crecv.at[h, 1], halo_send.at[h, 2], halo_recv.at[h, 2], left),
            remote(csend.at[h], crecv.at[h, 0], halo_send.at[h, 3], halo_recv.at[h, 3], right),
        ]

    pick_r, pick_l = row((16, XL)), lane((16, XL))

    def pick(base, kind):
        hot = ((pick_r == base) & (pick_l == 0)) | ((pick_r == base + 1) & (pick_l == XL - 1))
        return jnp.where(hot, 1.0, 0.0).astype(kind)

    def lookup(values):
        result = jnp.zeros(values.shape, F32)
        for label in range(16):
            result = jnp.where(values == label, table[label], result)
        return result

    for k in range(NZ):
        rsend[0, 0, k : k + 1, :] = vp_x[k, 8:9, :]
        rsend[0, 1, k : k + 1, :] = vp_x[k, 7 + ROWS : 8 + ROWS, :]
        rsend[0, 0, NZ + k : NZ + k + 1, :] = cls[k, 0:1, :].astype(F32)
        rsend[0, 1, NZ + k : NZ + k + 1, :] = cls[k, ROWS - 1 : ROWS, :].astype(F32)
    x_flat = vp_x[:, 8 : 8 + ROWS, :].reshape(NZ * ROWS, XL)
    cls_flat = cls[...].reshape(NZ * ROWS, XL).astype(F32)
    csend[0] = lax.dot_general(
        pick(0, F32), x_flat, NT, precision=HIGH, preferred_element_type=F32
    ) + lax.dot_general(
        pick(2, BF16), cls_flat.astype(BF16), NT, preferred_element_type=F32
    )
    copies = halo_copies(0)
    for copy in copies:
        copy.start()

    @pl.loop(0, NZ)
    def _(k):
        cp[k, 8 : 8 + ROWS, :] = lookup(cls[k])

    group, part = q // 4, lax.rem(q, 4)
    for half in range(2):
        cols = pl.ds(pl.multiple_of(group * 256 + half * 128, 128), 128)
        eigc[...] = jnp.broadcast_to(eig[:, cols], (128, 128)).T
        mine = eigc[pl.ds(pl.multiple_of(part * 32, 32), 32), 0:1] + shift[p]
        dinv[half * 32 : half * 32 + 32, :] = 1.0 / (mine + eig[...])

    has_up = jnp.where(q > 0, 1.0, 0.0).astype(F32)
    has_down = jnp.where(q < PY - 1, 1.0, 0.0).astype(F32)
    has_left = jnp.where(p > 0, 1.0, 0.0).astype(F32)
    has_right = jnp.where(p < PX - 1, 1.0, 0.0).astype(F32)

    place_r, place_l = row((16, XL)), lane((16, XL))

    def place(base, kind):
        hot_l = (place_r == base + 1) & (place_l == 0)
        hot_r = (place_r == base) & (place_l == XL - 1)
        return jnp.where(hot_l, 1.0, 0.0).astype(kind), jnp.where(hot_r, 1.0, 0.0).astype(kind)

    def wait_all(copies):
        for copy in copies:
            copy.wait_recv()

    def fill_rows(h, vp):
        for k in range(NZ):
            vp[k, 7:8, :] = rrecv[h, 0, k : k + 1, :] * has_up
            vp[k, 8 + ROWS : 9 + ROWS, :] = rrecv[h, 1, k : k + 1, :] * has_down

    wait_all(copies)
    fill_rows(0, vp_x)
    for k in range(NZ):
        cp[k, 7:8, :] = lookup(rrecv[0, 0, NZ + k : NZ + k + 1, :]) * has_up
        cp[k, 8 + ROWS : 9 + ROWS, :] = lookup(rrecv[0, 1, NZ + k : NZ + k + 1, :]) * has_down

    def columns(left, right, base, precision, kind):
        hot_l, hot_r = place(base, kind)
        out = lax.dot_general(
            (left * has_left).astype(kind), hot_l, TN, precision=precision, preferred_element_type=F32
        ) + lax.dot_general(
            (right * has_right).astype(kind), hot_r, TN, precision=precision, preferred_element_type=F32
        )
        return out.reshape(NZ, ROWS, XL)

    halo[...] = columns(crecv[0, 0], crecv[0, 1], 0, HIGH, F32)
    chalo[...] = columns(lookup(crecv[0, 0]), lookup(crecv[0, 1]), 2, HIGH, F32)

    lanes = lane((ROWS, XL))

    def east(values, edge):
        return jnp.where(lanes == XL - 1, edge, pltpu.roll(values, XL - 1, 1))

    def west(values, edge):
        return jnp.where(lanes == 0, edge, pltpu.roll(values, 1, 1))

    w_z[0] = jnp.zeros((ROWS, XL), F32)
    w_z[NZ] = jnp.zeros((ROWS, XL), F32)

    @pl.loop(0, NZ - 1)
    def _(k):
        w_z[k + 1] = 0.5 * (cp[k, 8 : 8 + ROWS, :] + cp[k + 1, 8 : 8 + ROWS, :])

    @pl.loop(0, NZ)
    def _(k):
        here = cp[k, 8 : 8 + ROWS, :]
        edge = chalo[k]
        to_e = 0.5 * (here + east(here, edge))
        to_w = 0.5 * (here + west(here, edge))
        to_n = 0.5 * (here + cp[k, 7 : 7 + ROWS, :])
        to_s = 0.5 * (here + cp[k, 9 : 9 + ROWS, :])
        w_e[k] = to_e
        w_w[k] = to_w
        w_n[k] = to_n
        w_s[k] = to_s
        w_sum[k] = to_e + to_w + to_n + to_s + w_z[k] + w_z[k + 1]

    def operator(vp, k):
        here = vp[k, 8 : 8 + ROWS, :]
        edge = halo[k]
        below = vp[jnp.maximum(k - 1, 0), 8 : 8 + ROWS, :]
        above = vp[jnp.minimum(k + 1, NZ - 1), 8 : 8 + ROWS, :]
        out = w_sum[k] * here - w_e[k] * east(here, edge) - w_w[k] * west(here, edge)
        out = out - w_n[k] * vp[k, 7 : 7 + ROWS, :] - w_s[k] * vp[k, 9 : 9 + ROWS, :]
        return here, out - w_z[k] * below - w_z[k + 1] * above

    def fold(values):
        part = values.reshape(values.shape[0] // 8, 8, values.shape[1]).sum(0)
        out = part[:, :128]
        for c in range(128, values.shape[1], 128):
            out = out + part[:, c : c + 128]
        return out

    def send_level(it, k):
        @pl.when(k != p)
        def _():
            remote(
                xsend.at[it, k], xrecv.at[it, p], a2a_send.at[it, 0], a2a_recv.at[it, 0], {"px": k}
            ).start()

        @pl.when(k == p)
        def _():
            xrecv[it, k] = xsend[it, k]

    def await_bytes(ref, sem):
        pltpu.make_async_copy(ref, ref, sem).wait()

    half_lane = lane((32, 128)) < 64

    def forward(it, gamma_prepare):
        await_bytes(xrecv.at[it, pl.ds(0, PX - 1)], a2a_recv.at[it, 0])
        for c in range(PX):
            lhs[:, c * XL : (c + 1) * XL] = xrecv[it, c]

        @pl.loop(0, G)
        def _(t):
            g = lax.rem(q // 4 + t, G)
            tile = jnp.dot(
                lhs[...],
                vec[:, pl.ds(pl.multiple_of(g * 256, 256), 256)],
                preferred_element_type=F32,
            )
            turned = jnp.concatenate([tile[:, :128], tile[:, 128:]], axis=0).T
            ysend[it, pl.ds(pl.multiple_of(g * 4, 4), 4)] = turned.astype(BF16).reshape(4, 32, 128)
            for h in range(4):
                dest = g * 4 + h

                @pl.when(dest != q)
                def _():
                    remote(
                        ysend.at[it, dest],
                        yrecv.at[it, q],
                        a2a_send.at[it, 1],
                        a2a_recv.at[it, 1],
                        {"py": dest},
                    ).start()

                @pl.when(dest == q)
                def _():
                    yrecv[it, q] = ysend[it, dest]

        gamma_prepare()
        await_bytes(yrecv.at[it, pl.ds(0, PY - 1)], a2a_recv.at[it, 1])
        for m in range(PY // 2):
            even, odd = yrecv[it, 2 * m].astype(F32), yrecv[it, 2 * m + 1].astype(F32)
            low = jnp.where(half_lane, even, pltpu.roll(odd, 64, 1))
            high = jnp.where(half_lane, pltpu.roll(even, 64, 1), odd)
            lhs[0:32, m * 128 : (m + 1) * 128] = low.astype(BF16)
            lhs[32:64, m * 128 : (m + 1) * 128] = high.astype(BF16)

    def second(it, alpha):
        def body(t, acc):
            cols = pl.ds(pl.multiple_of(t * 256, 256), 256)
            tile = jnp.dot(lhs[...], vec[:, cols], preferred_element_type=F32)
            if it == 0:
                s2[:, cols] = tile
            else:
                tile = s2[:, cols] - alpha * tile
            scaled = (tile * dinv[:, cols]).astype(BF16)
            s3[:, cols] = scaled
            return acc + fold(tile * scaled.astype(F32))

        return lax.fori_loop(0, G, body, jnp.zeros((8, 128), F32))

    def backward(it, between):
        @pl.loop(0, G)
        def _(t):
            g = lax.rem(q // 4 + t, G)
            tile = jnp.dot(
                s3[...],
                vec[:, pl.ds(pl.multiple_of(g * 256, 256), 256)],
                preferred_element_type=F32,
            )
            for h in range(2):
                low, high = tile[0:32, h * 128 : h * 128 + 128], tile[32:64, h * 128 : h * 128 + 128]
                even = jnp.where(half_lane, low, pltpu.roll(high, 64, 1))
                odd = jnp.where(half_lane, pltpu.roll(low, 64, 1), high)
                zsend[it, g * 4 + 2 * h] = even.astype(BF16)
                zsend[it, g * 4 + 2 * h + 1] = odd.astype(BF16)
            for h in range(4):
                dest = g * 4 + h

                @pl.when(dest != q)
                def _():
                    remote(
                        zsend.at[it, dest],
                        zrecv.at[it, q],
                        a2a_send.at[it, 2],
                        a2a_recv.at[it, 2],
                        {"py": dest},
                    ).start()

                @pl.when(dest == q)
                def _():
                    zrecv[it, q] = zsend[it, dest]

        between()
        await_bytes(zrecv.at[it, pl.ds(0, PY - 1)], a2a_recv.at[it, 2])
        for g in range(G):
            turned = zrecv[it, 4 * g : 4 * g + 4].reshape(128, 128).astype(F32).T.astype(BF16)
            lhs[:, g * 256 : g * 256 + 128] = turned[0:64]
            lhs[:, g * 256 + 128 : g * 256 + 256] = turned[64:128]

        @pl.loop(1, PX + 1)
        def _(t):
            c = lax.rem(p + t, PX)
            tile = jnp.dot(
                lhs[...],
                vec[:, pl.ds(pl.multiple_of(c * XL, XL), XL)],
                preferred_element_type=F32,
            )
            bsend[it, c] = tile.astype(BF16)

            @pl.when(c != p)
            def _():
                remote(
                    bsend.at[it, c],
                    brecv.at[it, p],
                    a2a_send.at[it, 3],
                    a2a_recv.at[it, 3],
                    {"px": c},
                ).start()

            @pl.when(c == p)
            def _():
                brecv[it, p] = bsend[it, c]

    def reduce_start(a, first, second_part):
        mine = jnp.concatenate(
            [first.sum(0, keepdims=True), second_part.sum(0, keepdims=True)], axis=1
        )
        arx_send[a, 0] = mine
        arx[a, p] = mine

        @pl.loop(1, PX)
        def _(t):
            dest = lax.rem(p + t, PX)
            remote(
                arx_send.at[a, 0], arx.at[a, p], ar_send.at[a, 0], ar_recv.at[a, 0], {"px": dest}
            ).start()

    def reduce_middle(a):
        await_bytes(arx.at[a, pl.ds(0, PX - 1)], ar_recv.at[a, 0])
        mine = arx[a, 0]
        for t in range(1, PX):
            mine = mine + arx[a, t]
        ary_send[a, 0] = mine
        ary[a, q] = mine

        @pl.loop(1, PY)
        def _(t):
            dest = lax.rem(q + t, PY)
            remote(
                ary_send.at[a, 0], ary.at[a, q], ar_send.at[a, 1], ar_recv.at[a, 1], {"py": dest}
            ).start()

    def reduce_end(a):
        await_bytes(ary.at[a, pl.ds(0, PY - 1)], ar_recv.at[a, 1])
        total = ary[a, 0]
        for t in range(1, PY):
            total = total + ary[a, t]
        return (
            total[:, :128].sum(1, keepdims=True),
            total[:, 128:].sum(1, keepdims=True),
        )

    zero = jnp.zeros((8, 128), F32)

    load_b.wait()

    @pl.loop(1, NZ + 1)
    def _(t):
        k = lax.rem(p + t, NZ)
        _, out = operator(vp_x, k)
        value = res[k] - out
        res[k] = value
        xsend[0, k] = value.astype(BF16)
        send_level(0, k)

    load_v.wait()

    def direction_halo(h, vp):
        for k in range(NZ):
            rsend[h, 0, k : k + 1, :] = vp[k, 8:9, :]
            rsend[h, 1, k : k + 1, :] = vp[k, 7 + ROWS : 8 + ROWS, :]
        flat = vp[:, 8 : 8 + ROWS, :].reshape(NZ * ROWS, XL).astype(BF16)
        csend[h] = lax.dot_general(pick(0, BF16), flat, NT, preferred_element_type=F32)
        copies = halo_copies(h)
        for copy in copies:
            copy.start()
        return copies

    def direction_edges(h, vp, copies):
        wait_all(copies)
        fill_rows(h, vp)
        halo[...] = columns(crecv[h, 0], crecv[h, 1], 0, None, BF16)

    forward(0, lambda: None)
    gamma_part = second(0, None)
    backward(0, lambda: None)
    await_bytes(brecv.at[0, pl.ds(0, PX - 1)], a2a_recv.at[0, 3])

    @pl.loop(0, NZ)
    def _(k):
        vp_0[k, 8 : 8 + ROWS, :] = brecv[0, k].astype(F32)

    direction_edges(1, vp_0, direction_halo(1, vp_0))

    def first_image(t, acc):
        k = lax.rem(p + t, NZ)
        here, out = operator(vp_0, k)
        image[k] = out
        xsend[1, k] = out.astype(BF16)
        send_level(1, k)
        return acc + fold(here * out)

    curve = lax.fori_loop(1, NZ + 1, first_image, zero)
    reduce_start(0, gamma_part, curve)

    forward(1, lambda: reduce_middle(0))
    gamma0, curve0 = reduce_end(0)
    alpha0 = gamma0 / curve0
    reduce_start(1, second(1, alpha0), zero)
    backward(1, lambda: reduce_middle(1))

    @pl.loop(0, NZ)
    def _(k):
        res[k] = res[k] - alpha0 * image[k]
        sol[k] = vp_x[k, 8 : 8 + ROWS, :] + alpha0 * vp_0[k, 8 : 8 + ROWS, :]

    gamma1, _ = reduce_end(1)
    beta = gamma1 / gamma0
    await_bytes(brecv.at[1, pl.ds(0, PX - 1)], a2a_recv.at[1, 3])

    @pl.loop(0, NZ)
    def _(k):
        value = brecv[1, k].astype(F32) + beta * vp_0[k, 8 : 8 + ROWS, :]
        vp_1[k, 8 : 8 + ROWS, :] = value
        direction[k] = value

    store_d = pltpu.make_async_copy(direction, dir_hbm, store_sem.at[0])
    store_d.start()
    direction_edges(2, vp_1, direction_halo(2, vp_1))

    def second_image(k, acc):
        here, out = operator(vp_1, k)
        image[k] = out
        return acc + fold(here * out)

    reduce_start(2, lax.fori_loop(0, NZ, second_image, zero), zero)
    reduce_middle(2)
    curve1, _ = reduce_end(2)
    alpha1 = gamma1 / curve1

    @pl.loop(0, NZ)
    def _(k):
        sol[k] = sol[k] + alpha1 * direction[k]
        res[k] = res[k] - alpha1 * image[k]

    store_x = pltpu.make_async_copy(sol, sol_hbm, store_sem.at[1])
    store_r = pltpu.make_async_copy(res, res_hbm, store_sem.at[2])
    store_x.start()
    store_r.start()

    for h in range(3):
        for copy in halo_copies(h):
            copy.wait_send()
    for it in range(2):
        await_bytes(xsend.at[it, pl.ds(0, PX - 1)], a2a_send.at[it, 0])
        await_bytes(ysend.at[it, pl.ds(0, PY - 1)], a2a_send.at[it, 1])
        await_bytes(zsend.at[it, pl.ds(0, PY - 1)], a2a_send.at[it, 2])
        await_bytes(bsend.at[it, pl.ds(0, PX - 1)], a2a_send.at[it, 3])
    for a in range(3):
        await_bytes(arx.at[a, pl.ds(0, PX - 1)], ar_send.at[a, 0])
        await_bytes(ary.at[a, pl.ds(0, PY - 1)], ar_send.at[a, 1])
    store_d.wait()
    store_x.wait()
    store_r.wait()


def scratch(PX, PY, XL, N):
    NZ = PX
    field = pltpu.VMEM((NZ, ROWS, XL), F32)
    padded = pltpu.VMEM((NZ, ROWS + 16, XL), F32)
    blocks = pltpu.VMEM((2, PX, ROWS, XL), BF16)
    tiles = pltpu.VMEM((2, PY, 32, 128), BF16)
    dma = pltpu.SemaphoreType.DMA
    return [
        pltpu.VMEM((N, N), BF16),
        pltpu.VMEM((NZ, ROWS, XL), jnp.int32),
        field,
        field,
        field,
        padded,
        padded,
        padded,
        padded,
        field,
        field,
        field,
        field,
        field,
        field,
        pltpu.VMEM((NZ + 1, ROWS, XL), F32),
        field,
        field,
        blocks,
        blocks,
        tiles,
        tiles,
        tiles,
        tiles,
        blocks,
        blocks,
        pltpu.VMEM((ROWS, N), BF16),
        pltpu.VMEM((ROWS, N), F32),
        pltpu.VMEM((ROWS, N), BF16),
        pltpu.VMEM((ROWS, N), F32),
        pltpu.VMEM((128, 128), F32),
        pltpu.VMEM((3, 2, 2 * NZ, XL), F32),
        pltpu.VMEM((3, 2, 2 * NZ, XL), F32),
        pltpu.VMEM((3, 16, NZ * ROWS), F32),
        pltpu.VMEM((3, 2, 16, NZ * ROWS), F32),
        pltpu.VMEM((3, 1, 1, 256), F32),
        pltpu.VMEM((3, PX, 1, 256), F32),
        pltpu.VMEM((3, 1, 1, 256), F32),
        pltpu.VMEM((3, PY, 1, 256), F32),
        dma((4,)),
        dma((3,)),
        dma((3, 4)),
        dma((3, 4)),
        dma((2, 4)),
        dma((2, 4)),
        dma((3, 2)),
        dma((3, 2)),
    ]


def shards(PX, PY, right_side, solution_in, classes, coeff_table, eigenvectors, eigenvalues, level_shift):
    XL, N = right_side.shape[2], eigenvectors.shape[0]
    out = jax.ShapeDtypeStruct(right_side.shape, F32)
    hbm = pl.BlockSpec(memory_space=pl.ANY)
    smem = pl.BlockSpec(memory_space=pltpu.SMEM)
    vmem = pl.BlockSpec(memory_space=pltpu.VMEM)
    return tuple(
        pl.pallas_call(
            functools.partial(kernel, PX, PY),
            out_shape=[out, out, out],
            in_specs=[hbm, hbm, hbm, smem, hbm, vmem, smem],
            out_specs=[hbm, hbm, hbm],
            scratch_shapes=scratch(PX, PY, XL, N),
            compiler_params=pltpu.CompilerParams(
                collective_id=0, has_side_effects=True, vmem_limit_bytes=50 * 2**20
            ),
        )(
            right_side,
            solution_in,
            classes,
            coeff_table,
            eigenvectors,
            eigenvalues.reshape(1, N),
            level_shift,
        )
    )


def solution(mesh):
    field = P(None, "py", "px")
    return jax.shard_map(
        functools.partial(shards, mesh.shape["px"], mesh.shape["py"]),
        mesh=mesh,
        in_specs=(field, field, field, P(), P(), P(), P()),
        out_specs=(field, field, field),
        check_vma=False,
    )
```

time: 578 us -> 121 us (0.21); the launches traced: 568 us -> 121 us
  blocking collectives: 328 us -> 0 us
  Pallas kernels: 0 us -> 113 us
  other arithmetic: 90.5 us -> 0 us
  starting transfers between devices: 42.3 us -> 0 us
  matrix products: 39.7 us -> 0 us
  waiting for transfers between devices: 32.3 us -> 0 us
  local copies, waits for them, and re-layouts: 29.7 us -> 7.5 us
    psum x3 -> x0, blocking collectives: 224 us -> none  [the longest x2 149 us: shards(): gamma = lax.psum(jnp.sum(residual * precond), ('px', 'py'))]
    pallas_call x0 -> x1, Pallas kernels: none -> 113 us  [shards(): pl.pallas_call(functools.partial(kernel, PX, PY), out_shape=[out, out, ou...]
    all_to_all x7 -> x0, blocking collectives: 104 us -> none  [the longest x2 33 us: precondition(): lax.all_to_all(rounded, 'px', split_axis=0, concat_axis=2, tiled=True)]
    unnamed x7 -> x0, other arithmetic: 69.2 us -> none
    dot_general x6 -> x0, matrix products: 39.7 us -> none  [the longest x2 21.1 us: precondition(): jnp.einsum('kji,yj->kyi', scaled, eigenvectors, preferred_element_type=jn...]
    ppermute x12 -> x0, starting transfers between devices: 33.5 us -> none  [the longest x6 22.9 us: padded_2(): before = lax.ppermute(last, axis, up)]
    ppermute x12 -> x0, waiting for transfers between devices: 24.1 us -> none  [the longest x6 19 us: padded_2(): after = lax.ppermute(initial, axis, down)]
    another operation x2 -> x0, other arithmetic: 12.2 us -> none  [shards(): jnp.stack((solution_in, coeff)).astype(jnp.bfloat16)]
  transfers between devices with their start and end apart: 13 -> 0, of which waited for: 10 -> 0; matrix products, arithmetic and copies ran while one was open for 0% -> 0% of each run, Pallas kernels for 0% -> 0%
where the time goes in v1:
time: 121 us
  Pallas kernels  113 us (93%)
  local copies, waits for them, and re-layouts  7.5 us (6%)
    pallas_call x1, Pallas kernels, shards(): pl.pallas_call(functools.partial(kernel, PX, PY), out_shape=[out, out, ou...  113 us
    unnamed x15, local copies, waits for them, and re-layouts  7.5 us

profile of v1, /device:TPU:1, one launch (start us, length us, event | category | flops | bytes accessed | tf_op | source)
XLA Modules:
  0.0 121.0 jit_solution(16148739407024708862)
XLA Ops:
  0.6 0.0 copy-start
  0.6 1.0 copy-done
  1.7 0.0 copy-start.1
  1.7 1.0 copy-done.1
  2.7 0.0 copy-start.2
  2.7 1.0 copy-done.2
  3.8 0.0 copy-start.3
  3.8 0.7 copy-done.3
  4.5 0.0 copy-start.4
  4.5 0.7 copy-done.4
  5.1 0.0 copy-start.5
  5.1 0.7 copy-done.5
  5.8 112.8 %shard_map.94 = (f32[8,64,256]{2,1,0:T(8,128)S(1)}, f32[8,64,256]{2,1,0:T(8,128)S(1)}, f32[8,64,256]{2,1,0:T(8,128)S(1)}) custom-call(f32[8,64,256]{2,1,0:T(8,128)S(1)} %copy-done, f32[8,64,256]{2,1,0:T(8,128)S(1)} %copy-done.1, s32[8,64,256]{2,1,0:T(8,128)S(1)} %copy-done.2, f32[16]{0:T(128)S(1)} %copy-done.4, bf16[2048,2048]{1,0:T(8,128)(2,1)} %vec_hbm.1, ...), custom_call_target="tpu_custom_call" | custom-call | tf_op jit(solution)/shard_map/pallas_call | solution.py:604
  118.6 0.8 copy.13
  119.4 0.8 copy.14
  120.2 0.8 copy.15
Async XLA Ops:
  0.6 1.0 copy-start
  1.7 1.0 copy-start.1
  2.7 1.0 copy-start.2
  3.8 0.7 copy-start.3
  4.5 0.7 copy-start.4
  5.1 0.7 copy-start.5

commit v2 on v0

v2 whole, which is shorter than its diff:
```python
import functools

import jax
import jax.numpy as jnp
from jax import lax
from jax.experimental import pallas as pl
from jax.experimental.pallas import tpu as pltpu
from jax.sharding import PartitionSpec as P

F32 = jnp.float32
BF16 = jnp.bfloat16
ROWS = 64
TOP, END = 8, 8 + ROWS
HIGH = lax.Precision.HIGHEST
NT = (((1,), (1,)), ((), ()))
TN = (((0,), (0,)), ((), ()))


def scratch(PX, PY, XL, N):
    NZ = PX
    field = pltpu.VMEM((NZ, ROWS, XL), F32)
    padded = pltpu.VMEM((NZ, ROWS + 16, XL), F32)
    lines = pltpu.VMEM((ROWS, N), F32)
    padded_lines = pltpu.VMEM((ROWS + 16, N), F32)
    tiles = pltpu.VMEM((2, PY, 32, 128), BF16)
    dma = pltpu.SemaphoreType.DMA
    return dict(
        vec=pltpu.VMEM((N, N), BF16),
        eig=pltpu.VMEM((1, N), F32),
        table=pltpu.SMEM((16,), F32),
        shift=pltpu.SMEM((NZ,), F32),
        cls=pltpu.VMEM((NZ, ROWS, XL), jnp.int32),
        sol=field,
        res=field,
        direction=field,
        image=field,
        vp_x=padded,
        vp_0=padded,
        vp_1=padded,
        cp=padded,
        halo=field,
        chalo=field,
        w_e=field,
        w_w=field,
        w_s=field,
        w_n=field,
        w_z=pltpu.VMEM((NZ + 1, ROWS, XL), F32),
        w_sum=field,
        cls_send=pltpu.VMEM((NZ + 2, ROWS, XL), BF16),
        cls_recv=pltpu.VMEM((PX, 3, ROWS, XL), BF16),
        pc=padded_lines,
        p_e=lines,
        p_w=lines,
        p_s=lines,
        p_n=lines,
        p_u=lines,
        p_d=lines,
        p_sum=lines,
        zp=pltpu.VMEM((2, ROWS + 16, N), F32),
        above=pltpu.VMEM((2, PX, ROWS, XL), BF16),
        below=pltpu.VMEM((2, PX, ROWS, XL), BF16),
        row_send=pltpu.VMEM((3, 2, 1, N), F32),
        row_recv=pltpu.VMEM((3, 2, 1, N), F32),
        xsend=pltpu.VMEM((PX, ROWS, XL), BF16),
        xrecv=pltpu.VMEM((PX, ROWS, XL), BF16),
        ysend=tiles,
        yrecv=tiles,
        zsend=tiles,
        zrecv=tiles,
        bsend=pltpu.VMEM((2, PX, ROWS, XL), BF16),
        brecv=pltpu.VMEM((2, PX, ROWS, XL), BF16),
        lhs=pltpu.VMEM((ROWS, N), BF16),
        s2=lines,
        s3=pltpu.VMEM((ROWS, N), BF16),
        dinv=lines,
        eigc=pltpu.VMEM((128, 128), F32),
        rsend=pltpu.VMEM((3, 2, 2 * NZ, XL), F32),
        rrecv=pltpu.VMEM((3, 2, 2 * NZ, XL), F32),
        csend=pltpu.VMEM((3, 8, NZ * ROWS), F32),
        crecv=pltpu.VMEM((3, 16, NZ * ROWS), F32),
        arx_send=pltpu.VMEM((3, 1, 1, 256), F32),
        arx=pltpu.VMEM((3, PX, 1, 256), F32),
        ary_send=pltpu.VMEM((3, 1, 1, 256), F32),
        ary=pltpu.VMEM((3, PY, 1, 256), F32),
        load_sem=dma((7,)),
        store_sem=dma((3,)),
        halo_send=dma((3, 4)),
        halo_recv=dma((3, 4)),
        cls_sem=dma((2,)),
        line_send=dma((3, 4)),
        line_recv=dma((3, 4)),
        a2a_send=dma((2, 4)),
        a2a_recv=dma((2, 4)),
        ar_send=dma((3, 2)),
        ar_recv=dma((3, 2)),
    )


def kernel(PX, PY, names, *refs):
    b_hbm, x_hbm, cls_hbm, table_hbm, vec_hbm, eig_hbm, shift_hbm, sol_hbm, res_hbm, dir_hbm = refs[:10]
    R = dict(zip(names, refs[10:]))
    vec, eig, table, shift, cls = (R[n] for n in ("vec", "eig", "table", "shift", "cls"))
    sol, res, direction, image = (R[n] for n in ("sol", "res", "direction", "image"))
    vp_x, vp_0, vp_1, cp, halo, chalo = (R[n] for n in ("vp_x", "vp_0", "vp_1", "cp", "halo", "chalo"))
    w_e, w_w, w_s, w_n, w_z, w_sum = (R[n] for n in ("w_e", "w_w", "w_s", "w_n", "w_z", "w_sum"))
    p_e, p_w, p_s, p_n, p_u, p_d, p_sum = (
        R[n] for n in ("p_e", "p_w", "p_s", "p_n", "p_u", "p_d", "p_sum")
    )
    cls_send, cls_recv, pc, zp = (R[n] for n in ("cls_send", "cls_recv", "pc", "zp"))
    above, below, row_send, row_recv = (R[n] for n in ("above", "below", "row_send", "row_recv"))
    xsend, xrecv, ysend, yrecv = (R[n] for n in ("xsend", "xrecv", "ysend", "yrecv"))
    zsend, zrecv, bsend, brecv = (R[n] for n in ("zsend", "zrecv", "bsend", "brecv"))
    lhs, s2, s3, dinv, eigc = (R[n] for n in ("lhs", "s2", "s3", "dinv", "eigc"))
    rsend, rrecv, csend, crecv = (R[n] for n in ("rsend", "rrecv", "csend", "crecv"))
    arx_send, arx, ary_send, ary = (R[n] for n in ("arx_send", "arx", "ary_send", "ary"))
    load_sem, store_sem, halo_send, halo_recv = (
        R[n] for n in ("load_sem", "store_sem", "halo_send", "halo_recv")
    )
    cls_sem, line_send, line_recv = (R[n] for n in ("cls_sem", "line_send", "line_recv"))
    a2a_send, a2a_recv, ar_send, ar_recv = (
        R[n] for n in ("a2a_send", "a2a_recv", "ar_send", "ar_recv")
    )

    NZ, XL, N = PX, image.shape[2], vec.shape[0]
    G = N // 256
    p, q = lax.axis_index("px"), lax.axis_index("py")
    pending = []
    far = sorted(range(1, PX), key=lambda t: -min(t, PX - t))

    def lane(shape):
        return lax.broadcasted_iota(jnp.int32, shape, len(shape) - 1)

    def row(shape):
        return lax.broadcasted_iota(jnp.int32, shape, len(shape) - 2)

    def block(i, size):
        return pl.ds(pl.multiple_of(i * size, size), size)

    def remote(src, dst, send, recv, where):
        return pltpu.make_async_remote_copy(
            src_ref=src, dst_ref=dst, send_sem=send, recv_sem=recv, device_id=where
        )

    def await_bytes(ref, sem):
        pltpu.make_async_copy(ref, ref, sem).wait()

    def sent_later(ref, sem):
        pending.append(lambda: await_bytes(ref, sem))

    north = {"py": lax.rem(q + PY - 1, PY)}
    south = {"py": lax.rem(q + 1, PY)}
    west_of = {"px": lax.rem(p + PX - 1, PX)}
    east_of = {"px": lax.rem(p + 1, PX)}
    has_north = jnp.where(q > 0, 1.0, 0.0).astype(F32)
    has_south = jnp.where(q < PY - 1, 1.0, 0.0).astype(F32)
    has_first = jnp.where(p > 0, 1.0, 0.0).astype(F32)
    has_last = jnp.where(p < PX - 1, 1.0, 0.0).astype(F32)

    load_cls = pltpu.make_async_copy(cls_hbm, cls, load_sem.at[0])
    load_x = pltpu.make_async_copy(x_hbm, vp_x.at[:, TOP:END, :], load_sem.at[1])
    load_b = pltpu.make_async_copy(b_hbm, res, load_sem.at[2])
    load_v = pltpu.make_async_copy(vec_hbm, vec, load_sem.at[3])
    load_t = pltpu.make_async_copy(table_hbm, table, load_sem.at[4])
    load_s = pltpu.make_async_copy(shift_hbm, shift, load_sem.at[5])
    load_e = pltpu.make_async_copy(eig_hbm, eig, load_sem.at[6])
    for load in (load_x, load_cls, load_t, load_s, load_e, load_b, load_v):
        load.start()

    barrier = pltpu.get_barrier_semaphore()

    @pl.loop(1, PX)
    def _(t):
        pl.semaphore_signal(barrier, inc=1, device_id={"px": lax.rem(p + t, PX)})

    @pl.loop(1, PY)
    def _(t):
        pl.semaphore_signal(barrier, inc=1, device_id={"py": lax.rem(q + t, PY)})

    def pick(base, kind, rows):
        r, l = row((rows, XL)), lane((rows, XL))
        hot = ((r == base) & (l == 0)) | ((r == base + 1) & (l == XL - 1))
        return jnp.where(hot, 1.0, 0.0).astype(kind)

    def place(base):
        r, l = row((16, XL)), lane((16, XL))
        hot_l = jnp.where((r == base + 1) & (l == 0), has_first, 0.0)
        hot_r = jnp.where((r == 8 + base) & (l == XL - 1), has_last, 0.0)
        return hot_l + hot_r

    def lookup(values):
        result = jnp.zeros(values.shape, F32)
        for label in range(16):
            result = jnp.where(values == label, table[label], result)
        return result

    def halo_copies(h):
        return [
            remote(rsend.at[h, 0], rrecv.at[h, 1], halo_send.at[h, 0], halo_recv.at[h, 0], north),
            remote(rsend.at[h, 1], rrecv.at[h, 0], halo_send.at[h, 1], halo_recv.at[h, 1], south),
            remote(csend.at[h], crecv.at[h, pl.ds(8, 8)], halo_send.at[h, 2], halo_recv.at[h, 2], west_of),
            remote(csend.at[h], crecv.at[h, pl.ds(0, 8)], halo_send.at[h, 3], halo_recv.at[h, 3], east_of),
        ]

    def start(copies):
        for copy in copies:
            copy.start()
            pending.append(copy.wait_send)
        return copies

    load_x.wait()
    load_cls.wait()
    for k in range(NZ):
        rsend[0, 0, k : k + 1, :] = vp_x[k, TOP : TOP + 1, :]
        rsend[0, 1, k : k + 1, :] = vp_x[k, END - 1 : END, :]
        rsend[0, 0, NZ + k : NZ + k + 1, :] = cls[k, 0:1, :].astype(F32)
        rsend[0, 1, NZ + k : NZ + k + 1, :] = cls[k, ROWS - 1 : ROWS, :].astype(F32)
    x_flat = vp_x[:, TOP:END, :].reshape(NZ * ROWS, XL)
    cls_flat = cls[...].reshape(NZ * ROWS, XL).astype(F32).astype(BF16)
    csend[0] = lax.dot_general(
        pick(0, F32, 8), x_flat, NT, precision=HIGH, preferred_element_type=F32
    ) + lax.dot_general(pick(2, BF16, 16), cls_flat, NT, preferred_element_type=F32)[0:8]
    cls_send[1 : NZ + 1] = cls_flat.reshape(NZ, ROWS, XL)
    cls_send[0] = jnp.zeros((ROWS, XL), BF16)
    cls_send[NZ + 1] = jnp.zeros((ROWS, XL), BF16)
    load_t.wait()
    load_s.wait()
    load_e.wait()
    pl.semaphore_wait(barrier, PX - 1 + PY - 1)
    copies = start(halo_copies(0))

    @pl.loop(0, NZ)
    def _(k):
        cp[k, TOP:END, :] = lookup(cls[k])

    w_z[0] = jnp.zeros((ROWS, XL), F32)
    w_z[NZ] = jnp.zeros((ROWS, XL), F32)

    @pl.loop(0, NZ - 1)
    def _(k):
        w_z[k + 1] = 0.5 * (cp[k, TOP:END, :] + cp[k + 1, TOP:END, :])

    group, part = q // 4, lax.rem(q, 4)
    for half in range(2):
        cols = pl.ds(pl.multiple_of(group * 256 + half * 128, 128), 128)
        eigc[...] = jnp.broadcast_to(eig[:, cols], (128, 128)).T
        mine = eigc[block(part, 32), 0:1] + shift[p]
        dinv[half * 32 : half * 32 + 32, :] = 1.0 / (mine + eig[...])

    def wait_all(copies):
        for copy in copies:
            copy.wait_recv()

    def fill_rows(h, vp):
        for k in range(NZ):
            vp[k, TOP - 1 : TOP, :] = rrecv[h, 0, k : k + 1, :] * has_north
            vp[k, END : END + 1, :] = rrecv[h, 1, k : k + 1, :] * has_south

    wait_all(copies)
    fill_rows(0, vp_x)
    for k in range(NZ):
        cp[k, TOP - 1 : TOP, :] = lookup(rrecv[0, 0, NZ + k : NZ + k + 1, :]) * has_north
        cp[k, END : END + 1, :] = lookup(rrecv[0, 1, NZ + k : NZ + k + 1, :]) * has_south

    def columns(values, base, precision, kind):
        out = lax.dot_general(
            values.astype(kind),
            place(base).astype(kind),
            TN,
            precision=precision,
            preferred_element_type=F32,
        )
        return out.reshape(NZ, ROWS, XL)

    halo[...] = columns(crecv[0], 0, HIGH, F32)
    chalo[...] = columns(lookup(crecv[0]), 2, HIGH, F32)

    lanes = lane((ROWS, XL))

    def east(values, edge):
        return jnp.where(lanes == XL - 1, edge, pltpu.roll(values, XL - 1, 1))

    def west(values, edge):
        return jnp.where(lanes == 0, edge, pltpu.roll(values, 1, 1))

    @pl.loop(0, NZ)
    def _(k):
        here = cp[k, TOP:END, :]
        edge = chalo[k]
        to_e = 0.5 * (here + east(here, edge))
        to_w = 0.5 * (here + west(here, edge))
        to_n = 0.5 * (here + cp[k, TOP - 1 : END - 1, :])
        to_s = 0.5 * (here + cp[k, TOP + 1 : END + 1, :])
        w_e[k] = to_e
        w_w[k] = to_w
        w_n[k] = to_n
        w_s[k] = to_s
        w_sum[k] = to_e + to_w + to_n + to_s + w_z[k] + w_z[k + 1]

    def operator(vp, k):
        here = vp[k, TOP:END, :]
        edge = halo[k]
        lower = vp[jnp.maximum(k - 1, 0), TOP:END, :]
        upper = vp[jnp.minimum(k + 1, NZ - 1), TOP:END, :]
        out = w_sum[k] * here - w_e[k] * east(here, edge) - w_w[k] * west(here, edge)
        out = out - w_n[k] * vp[k, TOP - 1 : END - 1, :] - w_s[k] * vp[k, TOP + 1 : END + 1, :]
        return out - w_z[k] * lower - w_z[k + 1] * upper

    def fold(values):
        part = values.reshape(values.shape[0] // 8, 8, values.shape[1]).sum(0)
        out = part[:, :128]
        for c in range(128, values.shape[1], 128):
            out = out + part[:, c : c + 128]
        return out

    load_b.wait()
    for t in far + [0]:
        k = lax.rem(p + t, NZ)
        value = res[k] - operator(vp_x, k)
        res[k] = value
        if t:
            xsend[k] = value.astype(BF16)
            remote(
                xsend.at[k], xrecv.at[p], a2a_send.at[0, 0], a2a_recv.at[0, 0], {"px": k}
            ).start()
        else:
            xrecv[p] = value.astype(BF16)
    sent_later(xsend.at[pl.ds(0, PX - 1)], a2a_send.at[0, 0])

    for t in far:
        dest = lax.rem(p + t, PX)
        remote(
            cls_send.at[pl.ds(dest, 3)], cls_recv.at[p], cls_sem.at[0], cls_sem.at[1], {"px": dest}
        ).start()
    cls_recv[p] = cls_send[pl.ds(p, 3)]
    sent_later(cls_recv.at[pl.ds(0, PX - 1)], cls_sem.at[0])

    load_v.wait()

    half_lane = lane((32, 128)) < 64

    def product(ref, cols):
        return jnp.dot(ref[...], vec[:, cols], preferred_element_type=F32)

    def scatter_tile(src, dst, it, which, t, g):
        for u in range(4):
            if t == 0 and u == 0:
                dst[it, q] = src[it, q]
                continue
            dest = g * 4 + (lax.rem(q + u, 4) if t == 0 else u)
            remote(
                src.at[it, dest], dst.at[it, q], a2a_send.at[it, which], a2a_recv.at[it, which], {"py": dest}
            ).start()

    def x_forward(it):
        for t in list(range(1, G)) + [0]:
            g = lax.rem(q // 4 + t, G)
            tile = product(lhs, block(g, 256))
            turned = jnp.concatenate([tile[:, :128], tile[:, 128:]], axis=0).T
            ysend[it, block(g, 4)] = turned.astype(BF16).reshape(4, 32, 128)
            scatter_tile(ysend, yrecv, it, 1, t, g)
        sent_later(ysend.at[it, pl.ds(0, PY - 1)], a2a_send.at[it, 1])

    def y_arrive(it):
        await_bytes(yrecv.at[it, pl.ds(0, PY - 1)], a2a_recv.at[it, 1])
        for m in range(PY // 2):
            even, odd = yrecv[it, 2 * m].astype(F32), yrecv[it, 2 * m + 1].astype(F32)
            low = jnp.where(half_lane, even, pltpu.roll(odd, 64, 1))
            high = jnp.where(half_lane, pltpu.roll(even, 64, 1), odd)
            lhs[0:32, m * 128 : (m + 1) * 128] = low.astype(BF16)
            lhs[32:64, m * 128 : (m + 1) * 128] = high.astype(BF16)

    def spectral(it, alpha):
        acc = jnp.zeros((8, 128), F32)
        for t in range(G):
            cols = slice(t * 256, (t + 1) * 256)
            tile = product(lhs, cols)
            if it == 0:
                s2[:, cols] = tile
            else:
                tile = s2[:, cols] - alpha * tile
            scaled = (tile * dinv[:, cols]).astype(BF16)
            s3[:, cols] = scaled
            acc = acc + fold(tile * scaled.astype(F32))
        return acc

    def y_back(it):
        for t in list(range(1, G)) + [0]:
            g = lax.rem(q // 4 + t, G)
            tile = product(s3, block(g, 256))
            for h in range(2):
                low, high = tile[0:32, h * 128 : h * 128 + 128], tile[32:64, h * 128 : h * 128 + 128]
                even = jnp.where(half_lane, low, pltpu.roll(high, 64, 1))
                odd = jnp.where(half_lane, pltpu.roll(low, 64, 1), high)
                zsend[it, g * 4 + 2 * h] = even.astype(BF16)
                zsend[it, g * 4 + 2 * h + 1] = odd.astype(BF16)
            scatter_tile(zsend, zrecv, it, 2, t, g)
        sent_later(zsend.at[it, pl.ds(0, PY - 1)], a2a_send.at[it, 2])

    def z_arrive(it):
        await_bytes(zrecv.at[it, pl.ds(0, PY - 1)], a2a_recv.at[it, 2])
        for g in range(G):
            turned = zrecv[it, 4 * g : 4 * g + 4].reshape(128, 128).astype(F32).T.astype(BF16)
            lhs[:, g * 256 : g * 256 + 128] = turned[0:64]
            lhs[:, g * 256 + 128 : g * 256 + 256] = turned[64:128]

    def line_copies(h):
        return [
            remote(row_send.at[h, 0], row_recv.at[h, 1], line_send.at[h, 0], line_recv.at[h, 0], north),
            remote(row_send.at[h, 1], row_recv.at[h, 0], line_send.at[h, 1], line_recv.at[h, 1], south),
        ]

    def x_back(it):
        for c in range(PX):
            tile = product(lhs, slice(c * XL, (c + 1) * XL)).astype(BF16)
            bsend[it, c] = tile
            zp[it, TOP:END, c * XL : (c + 1) * XL] = tile.astype(F32)
            remote(
                bsend.at[it, c], above.at[it, c], line_send.at[it, 2], line_recv.at[it, 2], west_of
            ).start()
            remote(
                bsend.at[it, c], below.at[it, c], line_send.at[it, 3], line_recv.at[it, 3], east_of
            ).start()
        row_send[it, 0] = zp[it, TOP : TOP + 1, :]
        row_send[it, 1] = zp[it, END - 1 : END, :]
        rows = start(line_copies(it))
        sent_later(bsend.at[it], line_send.at[it, 2])
        sent_later(bsend.at[it], line_send.at[it, 3])
        for t in far:
            c = lax.rem(p + t, PX)
            remote(
                bsend.at[it, c], brecv.at[it, p], a2a_send.at[it, 3], a2a_recv.at[it, 3], {"px": c}
            ).start()
        brecv[it, p] = bsend[it, p]
        sent_later(bsend.at[it, pl.ds(0, PX - 1)], a2a_send.at[it, 3])
        return rows

    def plane(which):
        return jnp.concatenate([cls_recv[c, which] for c in range(PX)], axis=1).astype(F32)

    def pencil_coefficients():
        await_bytes(cls_recv.at[pl.ds(0, PX - 1)], cls_sem.at[1])
        for c in range(PX):
            pc[TOP:END, c * XL : (c + 1) * XL] = lookup(cls_recv[c, 1].astype(F32))
        row_send[2, 0] = pc[TOP : TOP + 1, :]
        row_send[2, 1] = pc[END - 1 : END, :]
        rows = start(line_copies(2))
        for c in range(PX):
            cols = slice(c * XL, (c + 1) * XL)
            here = pc[TOP:END, cols]
            p_d[:, cols] = 0.5 * has_first * (here + lookup(cls_recv[c, 0].astype(F32)))
            p_u[:, cols] = 0.5 * has_last * (here + lookup(cls_recv[c, 2].astype(F32)))
        return rows

    wide = lane((16, N))

    def pencil_weights(rows):
        wait_all(rows)
        pc[TOP - 1 : TOP, :] = row_recv[2, 0] * has_north
        pc[END : END + 1, :] = row_recv[2, 1] * has_south
        for r in range(0, ROWS, 16):
            at = slice(r, r + 16)
            here = pc[TOP + r : TOP + r + 16, :]
            to_e = 0.5 * (here + jnp.where(wide == N - 1, 0.0, pltpu.roll(here, N - 1, 1)))
            to_w = 0.5 * (here + jnp.where(wide == 0, 0.0, pltpu.roll(here, 1, 1)))
            to_n = 0.5 * (here + pc[TOP - 1 + r : TOP + 15 + r, :])
            to_s = 0.5 * (here + pc[TOP + 1 + r : TOP + 17 + r, :])
            p_e[at, :] = jnp.where(wide == N - 1, 0.0, to_e)
            p_w[at, :] = jnp.where(wide == 0, 0.0, to_w)
            p_n[at, :] = to_n
            p_s[at, :] = to_s
            p_sum[at, :] = to_e + to_w + to_n + to_s + p_u[at, :] + p_d[at, :]

    def beside(ref, it, r):
        return jnp.concatenate([ref[it, c, r : r + 16, :] for c in range(PX)], axis=1).astype(F32)

    def pencil_operator(it, rows, beta):
        wait_all(rows)
        zp[it, TOP - 1 : TOP, :] = row_recv[it, 0] * has_north
        zp[it, END : END + 1, :] = row_recv[it, 1] * has_south
        if it == 1:
            for r in range(0, ROWS + 16, 16):
                if r == 0:
                    at = slice(TOP - 1, 16)
                elif r == ROWS:
                    at = slice(ROWS, END + 1)
                else:
                    at = slice(r, r + 16)
                zp[1, at, :] = zp[1, at, :] + beta * zp[0, at, :]
        await_bytes(above.at[it], line_recv.at[it, 2])
        await_bytes(below.at[it], line_recv.at[it, 3])
        acc = jnp.zeros((8, 128), F32)
        for r in range(0, ROWS, 16):
            at = slice(r, r + 16)
            here = zp[it, TOP + r : TOP + r + 16, :]
            up, down = beside(above, it, r), beside(below, it, r)
            if it == 1:
                up = up + beta * beside(above, 0, r)
                down = down + beta * beside(below, 0, r)
            out = p_sum[at, :] * here - p_e[at, :] * pltpu.roll(here, N - 1, 1)
            out = out - p_w[at, :] * pltpu.roll(here, 1, 1)
            out = out - p_n[at, :] * zp[it, TOP - 1 + r : TOP + 15 + r, :]
            out = out - p_s[at, :] * zp[it, TOP + 1 + r : TOP + 17 + r, :]
            out = out - p_u[at, :] * up - p_d[at, :] * down
            if it == 0:
                lhs[at, :] = out.astype(BF16)
            acc = acc + fold(here * out)
        return acc

    def reduce_start(a, first, second_part):
        mine = jnp.concatenate(
            [first.sum(0, keepdims=True), second_part.sum(0, keepdims=True)], axis=1
        )
        arx_send[a, 0] = mine
        arx[a, p] = mine
        for t in far:
            dest = lax.rem(p + t, PX)
            remote(
                arx_send.at[a, 0], arx.at[a, p], ar_send.at[a, 0], ar_recv.at[a, 0], {"px": dest}
            ).start()
        sent_later(arx.at[a, pl.ds(0, PX - 1)], ar_send.at[a, 0])

    def reduce_middle(a):
        await_bytes(arx.at[a, pl.ds(0, PX - 1)], ar_recv.at[a, 0])
        mine = arx[a, 0]
        for t in range(1, PX):
            mine = mine + arx[a, t]
        ary_send[a, 0] = mine
        ary[a, q] = mine

        @pl.loop(1, PY)
        def _(t):
            dest = lax.rem(q + t, PY)
            remote(
                ary_send.at[a, 0], ary.at[a, q], ar_send.at[a, 1], ar_recv.at[a, 1], {"py": dest}
            ).start()

        sent_later(ary.at[a, pl.ds(0, PY - 1)], ar_send.at[a, 1])

    def reduce_end(a):
        await_bytes(ary.at[a, pl.ds(0, PY - 1)], ar_recv.at[a, 1])
        total = ary[a, 0]
        for t in range(1, PY):
            total = total + ary[a, t]
        return (
            total[:, :128].sum(1, keepdims=True),
            total[:, 128:].sum(1, keepdims=True),
        )

    zero = jnp.zeros((8, 128), F32)

    def direction_halo(h, vp):
        for k in range(NZ):
            rsend[h, 0, k : k + 1, :] = vp[k, TOP : TOP + 1, :]
            rsend[h, 1, k : k + 1, :] = vp[k, END - 1 : END, :]
            rsend[h, :, NZ + k : NZ + k + 1, :] = jnp.zeros((2, 1, XL), F32)
        flat = vp[:, TOP:END, :].reshape(NZ * ROWS, XL).astype(BF16)
        csend[h] = lax.dot_general(pick(0, BF16, 16), flat, NT, preferred_element_type=F32)[0:8]
        return start(halo_copies(h))

    def direction_edges(h, vp, copies):
        wait_all(copies)
        fill_rows(h, vp)
        halo[...] = columns(crecv[h], 0, None, BF16)

    await_bytes(xrecv.at[pl.ds(0, PX - 1)], a2a_recv.at[0, 0])
    for c in range(PX):
        lhs[:, c * XL : (c + 1) * XL] = xrecv[c]
    x_forward(0)
    y_arrive(0)
    gamma_part = spectral(0, None)
    y_back(0)
    coeff_rows = pencil_coefficients()
    z_arrive(0)
    rows = x_back(0)
    pencil_weights(coeff_rows)
    curve = pencil_operator(0, rows, None)
    reduce_start(0, gamma_part, curve)

    x_forward(1)
    reduce_middle(0)
    await_bytes(brecv.at[0, pl.ds(0, PX - 1)], a2a_recv.at[0, 3])

    @pl.loop(0, NZ)
    def _(k):
        vp_0[k, TOP:END, :] = brecv[0, k].astype(F32)

    copies = direction_halo(1, vp_0)
    y_arrive(1)
    gamma0, curve0 = reduce_end(0)
    alpha0 = gamma0 / curve0
    reduce_start(1, spectral(1, alpha0), zero)
    y_back(1)
    direction_edges(1, vp_0, copies)

    @pl.loop(0, NZ)
    def _(k):
        res[k] = res[k] - alpha0 * operator(vp_0, k)
        sol[k] = vp_x[k, TOP:END, :] + alpha0 * vp_0[k, TOP:END, :]

    reduce_middle(1)
    z_arrive(1)
    rows = x_back(1)
    gamma1, _ = reduce_end(1)
    beta = gamma1 / gamma0
    reduce_start(2, pencil_operator(1, rows, beta), zero)

    await_bytes(brecv.at[1, pl.ds(0, PX - 1)], a2a_recv.at[1, 3])

    @pl.loop(0, NZ)
    def _(k):
        value = brecv[1, k].astype(F32) + beta * vp_0[k, TOP:END, :]
        vp_1[k, TOP:END, :] = value
        direction[k] = value

    copies = direction_halo(2, vp_1)
    store_d = pltpu.make_async_copy(direction, dir_hbm, store_sem.at[0])
    store_d.start()
    reduce_middle(2)
    direction_edges(2, vp_1, copies)

    @pl.loop(0, NZ)
    def _(k):
        image[k] = operator(vp_1, k)

    curve1, _ = reduce_end(2)
    alpha1 = gamma1 / curve1

    @pl.loop(0, NZ)
    def _(k):
        sol[k] = sol[k] + alpha1 * direction[k]
        res[k] = res[k] - alpha1 * image[k]

    store_x = pltpu.make_async_copy(sol, sol_hbm, store_sem.at[1])
    store_r = pltpu.make_async_copy(res, res_hbm, store_sem.at[2])
    store_x.start()
    store_r.start()

    for wait in pending:
        wait()
    store_d.wait()
    store_x.wait()
    store_r.wait()


def shards(PX, PY, right_side, solution_in, classes, coeff_table, eigenvectors, eigenvalues, level_shift):
    XL, N = right_side.shape[2], eigenvectors.shape[0]
    out = jax.ShapeDtypeStruct(right_side.shape, F32)
    hbm = pl.BlockSpec(memory_space=pl.ANY)
    buffers = scratch(PX, PY, XL, N)
    return tuple(
        pl.pallas_call(
            functools.partial(kernel, PX, PY, tuple(buffers)),
            out_shape=[out, out, out],
            in_specs=[hbm] * 7,
            out_specs=[hbm, hbm, hbm],
            scratch_shapes=list(buffers.values()),
            compiler_params=pltpu.CompilerParams(
                collective_id=0, has_side_effects=True, vmem_limit_bytes=60 * 2**20
            ),
        )(
            right_side,
            solution_in,
            classes,
            coeff_table,
            eigenvectors,
            eigenvalues.reshape(1, N),
            level_shift,
        )
    )


def solution(mesh):
    field = P(None, "py", "px")
    return jax.shard_map(
        functools.partial(shards, mesh.shape["px"], mesh.shape["py"]),
        mesh=mesh,
        in_specs=(field, field, field, P(), P(), P(), P()),
        out_specs=(field, field, field),
        check_vma=False,
    )
```

time: 578 us -> 110 us (0.19); the launches traced: 568 us -> 110 us
  blocking collectives: 328 us -> 0 us
  Pallas kernels: 0 us -> 104 us
  other arithmetic: 90.5 us -> 0 us
  starting transfers between devices: 42.3 us -> 0 us
  matrix products: 39.7 us -> 0 us
  waiting for transfers between devices: 32.3 us -> 0 us
  local copies, waits for them, and re-layouts: 29.7 us -> 5.6 us
    psum x3 -> x0, blocking collectives: 224 us -> none  [the longest x2 149 us: shards(): gamma = lax.psum(jnp.sum(residual * precond), ('px', 'py'))]
    all_to_all x7 -> x0, blocking collectives: 104 us -> none  [the longest x2 33 us: precondition(): lax.all_to_all(rounded, 'px', split_axis=0, concat_axis=2, tiled=True)]
    pallas_call x0 -> x1, Pallas kernels: none -> 104 us  [shards(): pl.pallas_call(functools.partial(kernel, PX, PY, tuple(buffers)), out_sha...]
    unnamed x7 -> x0, other arithmetic: 69.2 us -> none
    dot_general x6 -> x0, matrix products: 39.7 us -> none  [the longest x2 21.1 us: precondition(): jnp.einsum('kji,yj->kyi', scaled, eigenvectors, preferred_element_type=jn...]
    ppermute x12 -> x0, starting transfers between devices: 33.5 us -> none  [the longest x6 22.9 us: padded_2(): before = lax.ppermute(last, axis, up)]
    ppermute x12 -> x0, waiting for transfers between devices: 24.1 us -> none  [the longest x6 19 us: padded_2(): after = lax.ppermute(initial, axis, down)]
    another operation x2 -> x0, other arithmetic: 12.2 us -> none  [shards(): jnp.stack((solution_in, coeff)).astype(jnp.bfloat16)]
  transfers between devices with their start and end apart: 13 -> 0, of which waited for: 10 -> 0; matrix products, arithmetic and copies ran while one was open for 0% -> 0% of each run, Pallas kernels for 0% -> 0%
where the time goes in v2:
time: 110 us
  Pallas kernels  104 us (95%)
  local copies, waits for them, and re-layouts  5.6 us (5%)
    pallas_call x1, Pallas kernels, shards(): pl.pallas_call(functools.partial(kernel, PX, PY, tuple(buffers)), out_sha...  104 us
    unnamed x3, local copies, waits for them, and re-layouts  5.6 us

profile of v2, /device:TPU:1, one launch (start us, length us, event | category | flops | bytes accessed | tf_op | source)
XLA Modules:
  0.0 109.8 jit_solution(13112166223039347972)
XLA Ops:
  0.6 103.6 %shard_map.94 = (f32[8,64,256]{2,1,0:T(8,128)}, f32[8,64,256]{2,1,0:T(8,128)}, f32[8,64,256]{2,1,0:T(8,128)}) custom-call(f32[8,64,256]{2,1,0:T(8,128)} %refs_0_.1, f32[8,64,256]{2,1,0:T(8,128)} %refs_1_.1, s32[8,64,256]{2,1,0:T(8,128)} %refs_2_.1, f32[16]{0:T(128)} %refs_3_.1, bf16[2048,2048]{1,0:T(8,128)(2,1)} %refs_4_.1, f32[1,2048]{1,0:T(1,128)} %bitcast.1, ...), custom_call_target="tpu_custom_call" | custom-call | tf_op jit(solution)/shard_map/pallas_call | solution.py:651
  104.2 1.9 %copy.13 = f32[8,64,256]{2,1,0:T(8,128)} copy(f32[8,64,256]{2,1,0:T(8,128)} %get-tuple-element.6) | data formatting | bytes 1048576
  106.1 1.9 %copy.14 = f32[8,64,256]{2,1,0:T(8,128)} copy(f32[8,64,256]{2,1,0:T(8,128)} %get-tuple-element.7) | data formatting | bytes 1048576
  108.0 1.9 %copy.15 = f32[8,64,256]{2,1,0:T(8,128)} copy(f32[8,64,256]{2,1,0:T(8,128)} %get-tuple-element.8) | data formatting | bytes 1048576

commit v3 on v2

--- a/solution.py
+++ b/solution.py
@@ -46,8 +46,8 @@
         w_n=field,
         w_z=pltpu.VMEM((NZ + 1, ROWS, XL), F32),
         w_sum=field,
-        cls_send=pltpu.VMEM((NZ + 2, ROWS, XL), BF16),
-        cls_recv=pltpu.VMEM((PX, 3, ROWS, XL), BF16),
+        cls_send=pltpu.VMEM((NZ, ROWS, XL), BF16),
+        cls_recv=pltpu.VMEM((3, PX, ROWS, XL), BF16),
         pc=padded_lines,
         p_e=lines,
         p_w=lines,
@@ -74,19 +74,26 @@
         s3=pltpu.VMEM((ROWS, N), BF16),
         dinv=lines,
         eigc=pltpu.VMEM((128, 128), F32),
-        rsend=pltpu.VMEM((3, 2, 2 * NZ, XL), F32),
-        rrecv=pltpu.VMEM((3, 2, 2 * NZ, XL), F32),
-        csend=pltpu.VMEM((3, 8, NZ * ROWS), F32),
-        crecv=pltpu.VMEM((3, 16, NZ * ROWS), F32),
+        rsend=pltpu.VMEM((1, 2, 2 * NZ, XL), F32),
+        rrecv=pltpu.VMEM((1, 2, 2 * NZ, XL), F32),
+        csend=pltpu.VMEM((1, 8, NZ * ROWS), F32),
+        crecv=pltpu.VMEM((1, 16, NZ * ROWS), F32),
+        hrow_send=pltpu.VMEM((2, PX, 2, 1, XL), F32),
+        hrow_recv=pltpu.VMEM((2, PX, 2, 1, XL), F32),
+        edge_send=pltpu.VMEM((2, PX, 8, ROWS), F32),
+        edge_recv=pltpu.VMEM((2, PX, 8, ROWS), F32),
+        alpha_out=pltpu.VMEM((1, 128), F32),
         arx_send=pltpu.VMEM((3, 1, 1, 256), F32),
         arx=pltpu.VMEM((3, PX, 1, 256), F32),
         ary_send=pltpu.VMEM((3, 1, 1, 256), F32),
         ary=pltpu.VMEM((3, PY, 1, 256), F32),
         load_sem=dma((7,)),
-        store_sem=dma((3,)),
-        halo_send=dma((3, 4)),
-        halo_recv=dma((3, 4)),
-        cls_sem=dma((2,)),
+        store_sem=dma((5,)),
+        halo_send=dma((1, 4)),
+        halo_recv=dma((1, 4)),
+        grid_send=dma((2, 2)),
+        grid_recv=dma((2, 2)),
+        cls_sem=dma((2, 3)),
         line_send=dma((3, 4)),
         line_recv=dma((3, 4)),
         a2a_send=dma((2, 4)),
@@ -97,8 +104,9 @@
 
 
 def kernel(PX, PY, names, *refs):
-    b_hbm, x_hbm, cls_hbm, table_hbm, vec_hbm, eig_hbm, shift_hbm, sol_hbm, res_hbm, dir_hbm = refs[:10]
-    R = dict(zip(names, refs[10:]))
+    b_hbm, x_hbm, cls_hbm, table_hbm, vec_hbm, eig_hbm, shift_hbm = refs[:7]
+    sol_hbm, res_hbm, dir_hbm, image_hbm, alpha_hbm = refs[7:12]
+    R = dict(zip(names, refs[12:]))
     vec, eig, table, shift, cls = (R[n] for n in ("vec", "eig", "table", "shift", "cls"))
     sol, res, direction, image = (R[n] for n in ("sol", "res", "direction", "image"))
     vp_x, vp_0, vp_1, cp, halo, chalo = (R[n] for n in ("vp_x", "vp_0", "vp_1", "cp", "halo", "chalo"))
@@ -112,6 +120,18 @@
     zsend, zrecv, bsend, brecv = (R[n] for n in ("zsend", "zrecv", "bsend", "brecv"))
     lhs, s2, s3, dinv, eigc = (R[n] for n in ("lhs", "s2", "s3", "dinv", "eigc"))
     rsend, rrecv, csend, crecv = (R[n] for n in ("rsend", "rrecv", "csend", "crecv"))
+    hrow_send, hrow_recv, edge_send, edge_recv, grid_send, grid_recv, alpha_out = (
+        R[n]
+        for n in (
+            "hrow_send",
+            "hrow_recv",
+            "edge_send",
+            "edge_recv",
+            "grid_send",
+            "grid_recv",
+            "alpha_out",
+        )
+    )
     arx_send, arx, ary_send, ary = (R[n] for n in ("arx_send", "arx", "ary_send", "ary"))
     load_sem, store_sem, halo_send, halo_recv = (
         R[n] for n in ("load_sem", "store_sem", "halo_send", "halo_recv")
@@ -219,9 +239,7 @@
     csend[0] = lax.dot_general(
         pick(0, F32, 8), x_flat, NT, precision=HIGH, preferred_element_type=F32
     ) + lax.dot_general(pick(2, BF16, 16), cls_flat, NT, preferred_element_type=F32)[0:8]
-    cls_send[1 : NZ + 1] = cls_flat.reshape(NZ, ROWS, XL)
-    cls_send[0] = jnp.zeros((ROWS, XL), BF16)
-    cls_send[NZ + 1] = jnp.zeros((ROWS, XL), BF16)
+    cls_send[...] = cls_flat.reshape(NZ, ROWS, XL)
     load_t.wait()
     load_s.wait()
     load_e.wait()
@@ -327,12 +345,12 @@
     sent_later(xsend.at[pl.ds(0, PX - 1)], a2a_send.at[0, 0])
 
     for t in far:
-        dest = lax.rem(p + t, PX)
+        k = lax.rem(p + t, PX)
         remote(
-            cls_send.at[pl.ds(dest, 3)], cls_recv.at[p], cls_sem.at[0], cls_sem.at[1], {"px": dest}
+            cls_send.at[k], cls_recv.at[1, p], cls_sem.at[0, 1], cls_sem.at[1, 1], {"px": k}
         ).start()
-    cls_recv[p] = cls_send[pl.ds(p, 3)]
-    sent_later(cls_recv.at[pl.ds(0, PX - 1)], cls_sem.at[0])
+    cls_recv[1, p] = cls_send[p]
+    sent_later(cls_recv.at[1, pl.ds(0, PX - 1)], cls_sem.at[0, 1])
 
     load_v.wait()
 
@@ -425,36 +443,74 @@
         rows = start(line_copies(it))
         sent_later(bsend.at[it], line_send.at[it, 2])
         sent_later(bsend.at[it], line_send.at[it, 3])
+        return rows
+
+    def edges(it):
+        r, l = row((8 * PX, XL)), lane((8 * PX, XL))
+        out = jnp.zeros((8 * PX, ROWS), F32)
+        for c in range(PX):
+            hot = ((r == 8 * c + 8) & (l == XL - 1)) | ((r == 8 * c - 7) & (l == 0))
+            out = out + lax.dot_general(
+                jnp.where(hot, 1.0, 0.0).astype(BF16), bsend[it, c], NT, preferred_element_type=F32
+            )
+        edge_send[it] = out.reshape(PX, 8, ROWS)
+
+    def to_grid(it):
+        for c in range(PX):
+            cols = slice(c * XL, (c + 1) * XL)
+            hrow_send[it, c, 0] = zp[it, TOP - 1 : TOP, cols]
+            hrow_send[it, c, 1] = zp[it, END : END + 1, cols]
+        trio = (
+            (bsend, brecv, a2a_send.at[it, 3], a2a_recv.at[it, 3]),
+            (hrow_send, hrow_recv, grid_send.at[it, 0], grid_recv.at[it, 0]),
+            (edge_send, edge_recv, grid_send.at[it, 1], grid_recv.at[it, 1]),
+        )
         for t in far:
             c = lax.rem(p + t, PX)
-            remote(
-                bsend.at[it, c], brecv.at[it, p], a2a_send.at[it, 3], a2a_recv.at[it, 3], {"px": c}
-            ).start()
-        brecv[it, p] = bsend[it, p]
-        sent_later(bsend.at[it, pl.ds(0, PX - 1)], a2a_send.at[it, 3])
-        return rows
-
-    def plane(which):
-        return jnp.concatenate([cls_recv[c, which] for c in range(PX)], axis=1).astype(F32)
+            for src, dst, send, recv in trio:
+                remote(src.at[it, c], dst.at[it, p], send, recv, {"px": c}).start()
+        for src, dst, send, recv in trio:
+            dst[it, p] = src[it, p]
+            sent_later(src.at[it, pl.ds(0, PX - 1)], send)
+
+    def grid_arrive(it):
+        for dst, recv in (
+            (brecv, a2a_recv.at[it, 3]),
+            (hrow_recv, grid_recv.at[it, 0]),
+            (edge_recv, grid_recv.at[it, 1]),
+        ):
+            await_bytes(dst.at[it, pl.ds(0, PX - 1)], recv)
+
+    def plane_copies():
+        return [
+            remote(cls_recv.at[1], cls_recv.at[2], cls_sem.at[0, 2], cls_sem.at[1, 2], west_of),
+            remote(cls_recv.at[1], cls_recv.at[0], cls_sem.at[0, 0], cls_sem.at[1, 0], east_of),
+        ]
 
     def pencil_coefficients():
-        await_bytes(cls_recv.at[pl.ds(0, PX - 1)], cls_sem.at[1])
-        for c in range(PX):
-            pc[TOP:END, c * XL : (c + 1) * XL] = lookup(cls_recv[c, 1].astype(F32))
+        await_bytes(cls_recv.at[1, pl.ds(0, PX - 1)], cls_sem.at[1, 1])
+        planes = start(plane_copies())
+
+        @pl.loop(0, PX)
+        def _(c):
+            pc[TOP:END, block(c, XL)] = lookup(cls_recv[1, c].astype(F32))
+
         row_send[2, 0] = pc[TOP : TOP + 1, :]
         row_send[2, 1] = pc[END - 1 : END, :]
-        rows = start(line_copies(2))
-        for c in range(PX):
-            cols = slice(c * XL, (c + 1) * XL)
-            here = pc[TOP:END, cols]
-            p_d[:, cols] = 0.5 * has_first * (here + lookup(cls_recv[c, 0].astype(F32)))
-            p_u[:, cols] = 0.5 * has_last * (here + lookup(cls_recv[c, 2].astype(F32)))
-        return rows
+        return planes + start(line_copies(2))
 
     wide = lane((16, N))
 
     def pencil_weights(rows):
         wait_all(rows)
+
+        @pl.loop(0, PX)
+        def _(c):
+            cols = block(c, XL)
+            here = pc[TOP:END, cols]
+            p_d[:, cols] = 0.5 * has_first * (here + lookup(cls_recv[0, c].astype(F32)))
+            p_u[:, cols] = 0.5 * has_last * (here + lookup(cls_recv[2, c].astype(F32)))
+
         pc[TOP - 1 : TOP, :] = row_recv[2, 0] * has_north
         pc[END : END + 1, :] = row_recv[2, 1] * has_south
         for r in range(0, ROWS, 16):
@@ -474,9 +530,13 @@
         return jnp.concatenate([ref[it, c, r : r + 16, :] for c in range(PX)], axis=1).astype(F32)
 
     def pencil_operator(it, rows, beta):
+        edges(it)
         wait_all(rows)
         zp[it, TOP - 1 : TOP, :] = row_recv[it, 0] * has_north
         zp[it, END : END + 1, :] = row_recv[it, 1] * has_south
+        await_bytes(above.at[it], line_recv.at[it, 2])
+        await_bytes(below.at[it], line_recv.at[it, 3])
+        to_grid(it)
         if it == 1:
             for r in range(0, ROWS + 16, 16):
                 if r == 0:
@@ -486,8 +546,6 @@
                 else:
                     at = slice(r, r + 16)
                 zp[1, at, :] = zp[1, at, :] + beta * zp[0, at, :]
-        await_bytes(above.at[it], line_recv.at[it, 2])
-        await_bytes(below.at[it], line_recv.at[it, 3])
         acc = jnp.zeros((8, 128), F32)
         for r in range(0, ROWS, 16):
             at = slice(r, r + 16)
@@ -510,6 +568,23 @@
         mine = jnp.concatenate(
             [first.sum(0, keepdims=True), second_part.sum(0, keepdims=True)], axis=1
         )
+        ary_send[a, 0] = mine
+        ary[a, q] = mine
+
+        @pl.loop(1, PY)
+        def _(t):
+            dest = lax.rem(q + t, PY)
+            remote(
+                ary_send.at[a, 0], ary.at[a, q], ar_send.at[a, 1], ar_recv.at[a, 1], {"py": dest}
+            ).start()
+
+        sent_later(ary.at[a, pl.ds(0, PY - 1)], ar_send.at[a, 1])
+
+    def reduce_middle(a):
+        await_bytes(ary.at[a, pl.ds(0, PY - 1)], ar_recv.at[a, 1])
+        mine = ary[a, 0]
+        for t in range(1, PY):
+            mine = mine + ary[a, t]
         arx_send[a, 0] = mine
         arx[a, p] = mine
         for t in far:
@@ -519,28 +594,11 @@
             ).start()
         sent_later(arx.at[a, pl.ds(0, PX - 1)], ar_send.at[a, 0])
 
-    def reduce_middle(a):
+    def reduce_end(a):
         await_bytes(arx.at[a, pl.ds(0, PX - 1)], ar_recv.at[a, 0])
-        mine = arx[a, 0]
+        total = arx[a, 0]
         for t in range(1, PX):
-            mine = mine + arx[a, t]
-        ary_send[a, 0] = mine
-        ary[a, q] = mine
-
-        @pl.loop(1, PY)
-        def _(t):
-            dest = lax.rem(q + t, PY)
-            remote(
-                ary_send.at[a, 0], ary.at[a, q], ar_send.at[a, 1], ar_recv.at[a, 1], {"py": dest}
-            ).start()
-
-        sent_later(ary.at[a, pl.ds(0, PY - 1)], ar_send.at[a, 1])
-
-    def reduce_end(a):
-        await_bytes(ary.at[a, pl.ds(0, PY - 1)], ar_recv.at[a, 1])
-        total = ary[a, 0]
-        for t in range(1, PY):
-            total = total + ary[a, t]
+            total = total + arx[a, t]
         return (
             total[:, :128].sum(1, keepdims=True),
             total[:, 128:].sum(1, keepdims=True),
@@ -548,55 +606,69 @@
 
     zero = jnp.zeros((8, 128), F32)
 
-    def direction_halo(h, vp):
+    place_r, place_l = row((8, XL)), lane((8, XL))
+    outside = jnp.where(
+        ((place_r == 0) & (place_l == 0)) | ((place_r == 1) & (place_l == XL - 1)), 1.0, 0.0
+    )
+
+    def grid_direction(it, vp, beta):
+        def mixed(ref, k):
+            return ref[0, k] if it == 0 else ref[1, k] + beta * ref[0, k]
+
         for k in range(NZ):
-            rsend[h, 0, k : k + 1, :] = vp[k, TOP : TOP + 1, :]
-            rsend[h, 1, k : k + 1, :] = vp[k, END - 1 : END, :]
-            rsend[h, :, NZ + k : NZ + k + 1, :] = jnp.zeros((2, 1, XL), F32)
-        flat = vp[:, TOP:END, :].reshape(NZ * ROWS, XL).astype(BF16)
-        csend[h] = lax.dot_general(pick(0, BF16, 16), flat, NT, preferred_element_type=F32)[0:8]
-        return start(halo_copies(h))
-
-    def direction_edges(h, vp, copies):
-        wait_all(copies)
-        fill_rows(h, vp)
-        halo[...] = columns(crecv[h], 0, None, BF16)
+            around = mixed(hrow_recv, k)
+            vp[k, TOP - 1 : TOP, :] = around[0]
+            vp[k, END : END + 1, :] = around[1]
+            halo[k] = lax.dot_general(
+                mixed(edge_recv, k), outside, TN, precision=HIGH, preferred_element_type=F32
+            )
+
+        @pl.loop(0, NZ)
+        def _(k):
+            value = brecv[it, k].astype(F32)
+            if it == 1:
+                value = value + beta * vp_0[k, TOP:END, :]
+                direction[k] = value
+            vp[k, TOP:END, :] = value
 
     await_bytes(xrecv.at[pl.ds(0, PX - 1)], a2a_recv.at[0, 0])
     for c in range(PX):
         lhs[:, c * XL : (c + 1) * XL] = xrecv[c]
     x_forward(0)
+    coeff_rows = pencil_coefficients()
     y_arrive(0)
     gamma_part = spectral(0, None)
     y_back(0)
-    coeff_rows = pencil_coefficients()
+    pencil_weights(coeff_rows)
     z_arrive(0)
     rows = x_back(0)
-    pencil_weights(coeff_rows)
     curve = pencil_operator(0, rows, None)
     reduce_start(0, gamma_part, curve)
 
     x_forward(1)
     reduce_middle(0)
-    await_bytes(brecv.at[0, pl.ds(0, PX - 1)], a2a_recv.at[0, 3])
+    grid_arrive(0)
+    grid_direction(0, vp_0, None)
 
     @pl.loop(0, NZ)
     def _(k):
-        vp_0[k, TOP:END, :] = brecv[0, k].astype(F32)
-
-    copies = direction_halo(1, vp_0)
+        image[k] = operator(vp_0, k)
+
     y_arrive(1)
     gamma0, curve0 = reduce_end(0)
     alpha0 = gamma0 / curve0
     reduce_start(1, spectral(1, alpha0), zero)
     y_back(1)
-    direction_edges(1, vp_0, copies)
 
     @pl.loop(0, NZ)
     def _(k):
-        res[k] = res[k] - alpha0 * operator(vp_0, k)
+        res[k] = res[k] - alpha0 * image[k]
         sol[k] = vp_x[k, TOP:END, :] + alpha0 * vp_0[k, TOP:END, :]
 
+    store_x = pltpu.make_async_copy(sol, sol_hbm, store_sem.at[0])
+    store_r = pltpu.make_async_copy(res, res_hbm, store_sem.at[1])
+    store_x.start()
+    store_r.start()
     reduce_middle(1)
     z_arrive(1)
     rows = x_back(1)
@@ -604,42 +676,37 @@
     beta = gamma1 / gamma0
     reduce_start(2, pencil_operator(1, rows, beta), zero)
 
-    await_bytes(brecv.at[1, pl.ds(0, PX - 1)], a2a_recv.at[1, 3])
-
-    @pl.loop(0, NZ)
-    def _(k):
-        value = brecv[1, k].astype(F32) + beta * vp_0[k, TOP:END, :]
-        vp_1[k, TOP:END, :] = value
-        direction[k] = value
-
-    copies = direction_halo(2, vp_1)
-    store_d = pltpu.make_async_copy(direction, dir_hbm, store_sem.at[0])
+    reduce_middle(2)
+    grid_arrive(1)
+    grid_direction(1, vp_1, beta)
+    store_d = pltpu.make_async_copy(direction, dir_hbm, store_sem.at[2])
     store_d.start()
-    reduce_middle(2)
-    direction_edges(2, vp_1, copies)
 
     @pl.loop(0, NZ)
     def _(k):
         image[k] = operator(vp_1, k)
 
+    store_i = pltpu.make_async_copy(image, image_hbm, store_sem.at[3])
+    store_i.start()
     curve1, _ = reduce_end(2)
-    alpha1 = gamma1 / curve1
-
-    @pl.loop(0, NZ)
-    def _(k):
-        sol[k] = sol[k] + alpha1 * direction[k]
-        res[k] = res[k] - alpha1 * image[k]
-
-    store_x = pltpu.make_async_copy(sol, sol_hbm, store_sem.at[1])
-    store_r = pltpu.make_async_copy(res, res_hbm, store_sem.at[2])
-    store_x.start()
-    store_r.start()
+    alpha_out[...] = jnp.broadcast_to(gamma1 / curve1, (1, 128))
+    store_a = pltpu.make_async_copy(alpha_out, alpha_hbm, store_sem.at[4])
+    store_a.start()
 
     for wait in pending:
         wait()
-    store_d.wait()
     store_x.wait()
     store_r.wait()
+    store_d.wait()
+    store_i.wait()
+    store_a.wait()
+
+
+def last_update(alpha, x, r, d, image, sol, res, direction):
+    step = alpha[0:1, 0:1]
+    sol[...] = x[...] + step * d[...]
+    res[...] = r[...] - step * image[...]
+    direction[...] = d[...]
 
 
 def shards(PX, PY, right_side, solution_in, classes, coeff_table, eigenvectors, eigenvalues, level_shift):
@@ -647,25 +714,33 @@
     out = jax.ShapeDtypeStruct(right_side.shape, F32)
     hbm = pl.BlockSpec(memory_space=pl.ANY)
     buffers = scratch(PX, PY, XL, N)
+    x, r, d, image, alpha = pl.pallas_call(
+        functools.partial(kernel, PX, PY, tuple(buffers)),
+        out_shape=[out] * 4 + [jax.ShapeDtypeStruct((1, 128), F32)],
+        in_specs=[hbm] * 7,
+        out_specs=[hbm] * 5,
+        scratch_shapes=list(buffers.values()),
+        compiler_params=pltpu.CompilerParams(
+            collective_id=0, has_side_effects=True, vmem_limit_bytes=60 * 2**20
+        ),
+    )(
+        right_side,
+        solution_in,
+        classes,
+        coeff_table,
+        eigenvectors,
+        eigenvalues.reshape(1, N),
+        level_shift,
+    )
+    levels = pl.BlockSpec((2, ROWS, XL), lambda k: (k, 0, 0))
     return tuple(
         pl.pallas_call(
-            functools.partial(kernel, PX, PY, tuple(buffers)),
-            out_shape=[out, out, out],
-            in_specs=[hbm] * 7,
-            out_specs=[hbm, hbm, hbm],
-            scratch_shapes=list(buffers.values()),
-            compiler_params=pltpu.CompilerParams(
-                collective_id=0, has_side_effects=True, vmem_limit_bytes=60 * 2**20
-            ),
-        )(
-            right_side,
-            solution_in,
-            classes,
-            coeff_table,
-            eigenvectors,
-            eigenvalues.reshape(1, N),
-            level_shift,
-        )
+            last_update,
+            grid=(PX // 2,),
+            out_shape=[out] * 3,
+            in_specs=[pl.BlockSpec((1, 128), lambda k: (0, 0))] + [levels] * 4,
+            out_specs=[levels] * 3,
+        )(alpha, x, r, d, image)
     )
 
 

time: 110 us -> 97 us (0.88)
  Pallas kernels: 104 us -> 96.2 us
  local copies, waits for them, and re-layouts: 5.6 us -> 0 us
    pallas_call x1, Pallas kernels: 104 us -> 92.4 us  [shards(): pl.pallas_call(functools.partial(kernel, PX, PY, tuple(buffers)), out_sha...]
    unnamed x3 -> x0, local copies, waits for them, and re-layouts: 5.6 us -> none
    pallas_call x0 -> x1, Pallas kernels: none -> 3.84 us  [shards(): pl.pallas_call(last_update, grid=(PX // 2,), out_shape=[out] * 3, in_spec...]
where the time goes in v3:
time: 97 us; the launch traced here: 96.9 us
  Pallas kernels  96.2 us (99%)
    pallas_call x1, Pallas kernels, shards(): pl.pallas_call(functools.partial(kernel, PX, PY, tuple(buffers)), out_sha...  92.4 us
    pallas_call x1, Pallas kernels, shards(): pl.pallas_call(last_update, grid=(PX // 2,), out_shape=[out] * 3, in_spec...  3.84 us

profile of v3, /device:TPU:1, one launch (start us, length us, event | category | flops | bytes accessed | tf_op | source)
XLA Modules:
  0.0 96.9 jit_solution(13614269519882707409)
XLA Ops:
  0.6 92.4 %shard_map.94 = (f32[8,64,256]{2,1,0:T(8,128)}, f32[8,64,256]{2,1,0:T(8,128)}, f32[8,64,256]{2,1,0:T(8,128)}, f32[8,64,256]{2,1,0:T(8,128)}, f32[1,128]{1,0:T(1,128)}) custom-call(f32[8,64,256]{2,1,0:T(8,128)} %refs_0_.1, f32[8,64,256]{2,1,0:T(8,128)} %refs_1_.1, s32[8,64,256]{2,1,0:T(8,128)} %refs_2_.1, f32[16]{0:T(128)} %refs_3_.1, ...), custom_call_target="tpu_custom_call" | custom-call | tf_op jit(solution)/shard_map/pallas_call | solution.py:717
  93.0 3.8 %shard_map.95 = (f32[8,64,256]{2,1,0:T(8,128)}, f32[8,64,256]{2,1,0:T(8,128)}, f32[8,64,256]{2,1,0:T(8,128)}) custom-call(f32[1,128]{1,0:T(1,128)} %get-tuple-element.8.alpha, f32[8,64,256]{2,1,0:T(8,128)} %get-tuple-element.9.x, f32[8,64,256]{2,1,0:T(8,128)} %get-tuple-element.10.r, f32[8,64,256]{2,1,0:T(8,128)} %get-tuple-element.11.d, ...), custom_call_target="tpu_custom_call" | custom-call | tf_op jit(solution)/shard_map/pallas_call | solution.py:737

commit v4 on v3

--- a/solution.py
+++ b/solution.py
@@ -70,6 +70,9 @@
         bsend=pltpu.VMEM((2, PX, ROWS, XL), BF16),
         brecv=pltpu.VMEM((2, PX, ROWS, XL), BF16),
         lhs=pltpu.VMEM((ROWS, N), BF16),
+        acc=lines,
+        inner=lines,
+        image_0=lines,
         s2=lines,
         s3=pltpu.VMEM((ROWS, N), BF16),
         dinv=lines,
@@ -97,7 +100,7 @@
         line_send=dma((3, 4)),
         line_recv=dma((3, 4)),
         a2a_send=dma((2, 4)),
-        a2a_recv=dma((2, 4)),
+        a2a_recv=dma((2, 4, 8)),
         ar_send=dma((3, 2)),
         ar_recv=dma((3, 2)),
     )
@@ -119,6 +122,7 @@
     xsend, xrecv, ysend, yrecv = (R[n] for n in ("xsend", "xrecv", "ysend", "yrecv"))
     zsend, zrecv, bsend, brecv = (R[n] for n in ("zsend", "zrecv", "bsend", "brecv"))
     lhs, s2, s3, dinv, eigc = (R[n] for n in ("lhs", "s2", "s3", "dinv", "eigc"))
+    acc, inner, image_0 = (R[n] for n in ("acc", "inner", "image_0"))
     rsend, rrecv, csend, crecv = (R[n] for n in ("rsend", "rrecv", "csend", "crecv"))
     hrow_send, hrow_recv, edge_send, edge_recv, grid_send, grid_recv, alpha_out = (
         R[n]
@@ -146,6 +150,7 @@
     p, q = lax.axis_index("px"), lax.axis_index("py")
     pending = []
     far = sorted(range(1, PX), key=lambda t: -min(t, PX - t))
+    far_groups = sorted(range(G), key=lambda t: -min(t, G - t))
 
     def lane(shape):
         return lax.broadcasted_iota(jnp.int32, shape, len(shape) - 1)
@@ -208,10 +213,12 @@
         return hot_l + hot_r
 
     def lookup(values):
-        result = jnp.zeros(values.shape, F32)
-        for label in range(16):
-            result = jnp.where(values == label, table[label], result)
-        return result
+        picks = values.astype(jnp.int32)
+        level = [table[label] for label in range(16)]
+        for bit in range(4):
+            odd = (picks & (1 << bit)) != 0
+            level = [jnp.where(odd, level[i + 1], level[i]) for i in range(0, len(level), 2)]
+        return level[0]
 
     def halo_copies(h):
         return [
@@ -236,9 +243,10 @@
         rsend[0, 1, NZ + k : NZ + k + 1, :] = cls[k, ROWS - 1 : ROWS, :].astype(F32)
     x_flat = vp_x[:, TOP:END, :].reshape(NZ * ROWS, XL)
     cls_flat = cls[...].reshape(NZ * ROWS, XL).astype(F32).astype(BF16)
-    csend[0] = lax.dot_general(
-        pick(0, F32, 8), x_flat, NT, precision=HIGH, preferred_element_type=F32
-    ) + lax.dot_general(pick(2, BF16, 16), cls_flat, NT, preferred_element_type=F32)[0:8]
+    csend[0] = (
+        lax.dot_general(pick(0, BF16, 16), x_flat.astype(BF16), NT, preferred_element_type=F32)
+        + lax.dot_general(pick(2, BF16, 16), cls_flat, NT, preferred_element_type=F32)
+    )[0:8]
     cls_send[...] = cls_flat.reshape(NZ, ROWS, XL)
     load_t.wait()
     load_s.wait()
@@ -257,13 +265,6 @@
     def _(k):
         w_z[k + 1] = 0.5 * (cp[k, TOP:END, :] + cp[k + 1, TOP:END, :])
 
-    group, part = q // 4, lax.rem(q, 4)
-    for half in range(2):
-        cols = pl.ds(pl.multiple_of(group * 256 + half * 128, 128), 128)
-        eigc[...] = jnp.broadcast_to(eig[:, cols], (128, 128)).T
-        mine = eigc[block(part, 32), 0:1] + shift[p]
-        dinv[half * 32 : half * 32 + 32, :] = 1.0 / (mine + eig[...])
-
     def wait_all(copies):
         for copy in copies:
             copy.wait_recv()
@@ -275,22 +276,28 @@
 
     wait_all(copies)
     fill_rows(0, vp_x)
+    north_row = lookup(rrecv[0, 0, NZ : 2 * NZ, :]) * has_north
+    south_row = lookup(rrecv[0, 1, NZ : 2 * NZ, :]) * has_south
     for k in range(NZ):
-        cp[k, TOP - 1 : TOP, :] = lookup(rrecv[0, 0, NZ + k : NZ + k + 1, :]) * has_north
-        cp[k, END : END + 1, :] = lookup(rrecv[0, 1, NZ + k : NZ + k + 1, :]) * has_south
-
-    def columns(values, base, precision, kind):
+        cp[k, TOP - 1 : TOP, :] = north_row[k : k + 1]
+        cp[k, END : END + 1, :] = south_row[k : k + 1]
+
+    def columns(values, base):
+        high = values.astype(BF16)
+        rest = values - high.astype(F32)
+        middle = rest.astype(BF16)
+        low = (rest - middle.astype(F32)).astype(BF16)
+        hot = place(base).astype(BF16)
         out = lax.dot_general(
-            values.astype(kind),
-            place(base).astype(kind),
+            jnp.concatenate([high, middle, low], axis=0),
+            jnp.concatenate([hot, hot, hot], axis=0),
             TN,
-            precision=precision,
             preferred_element_type=F32,
         )
         return out.reshape(NZ, ROWS, XL)
 
-    halo[...] = columns(crecv[0], 0, HIGH, F32)
-    chalo[...] = columns(lookup(crecv[0]), 2, HIGH, F32)
+    halo[...] = columns(crecv[0], 0)
+    chalo[...] = columns(lookup(crecv[0]), 2)
 
     lanes = lane((ROWS, XL))
 
@@ -338,26 +345,42 @@
         if t:
             xsend[k] = value.astype(BF16)
             remote(
-                xsend.at[k], xrecv.at[p], a2a_send.at[0, 0], a2a_recv.at[0, 0], {"px": k}
+                xsend.at[k], xrecv.at[p], a2a_send.at[0, 0], a2a_recv.at[0, 0, p], {"px": k}
             ).start()
         else:
             xrecv[p] = value.astype(BF16)
     sent_later(xsend.at[pl.ds(0, PX - 1)], a2a_send.at[0, 0])
 
-    for t in far:
-        k = lax.rem(p + t, PX)
-        remote(
-            cls_send.at[k], cls_recv.at[1, p], cls_sem.at[0, 1], cls_sem.at[1, 1], {"px": k}
-        ).start()
-    cls_recv[1, p] = cls_send[p]
-    sent_later(cls_recv.at[1, pl.ds(0, PX - 1)], cls_sem.at[0, 1])
+    group, part = q // 4, lax.rem(q, 4)
+    for half in range(2):
+        cols = pl.ds(pl.multiple_of(group * 256 + half * 128, 128), 128)
+        eigc[...] = jnp.broadcast_to(eig[:, cols], (128, 128)).T
+        mine = eigc[block(part, 32), 0:1] + shift[p]
+        dinv[half * 32 : half * 32 + 32, :] = 1.0 / (mine + eig[...])
 
     load_v.wait()
 
     half_lane = lane((32, 128)) < 64
-
-    def product(ref, cols):
-        return jnp.dot(ref[...], vec[:, cols], preferred_element_type=F32)
+    own_group = q // 4
+
+    def product(ref, rows, cols):
+        return jnp.dot(ref[:, rows], vec[rows, cols], preferred_element_type=F32)
+
+    def in_steps(parts, size, fetch, consume, order):
+        steps = [parts[i : i + 2] for i in range(0, len(parts), 2)]
+        for i, step in enumerate(steps):
+            rows = [block(fetch(t), size) for t in step]
+            for n in order:
+                cols = block(n, 256)
+                tile = product(lhs, rows[0], cols)
+                for r in rows[1:]:
+                    tile = tile + product(lhs, r, cols)
+                if i:
+                    tile = acc[:, cols] + tile
+                if i == len(steps) - 1:
+                    consume(n, tile)
+                else:
+                    acc[:, cols] = tile
 
     def scatter_tile(src, dst, it, which, t, g):
         for u in range(4):
@@ -366,60 +389,93 @@
                 continue
             dest = g * 4 + (lax.rem(q + u, 4) if t == 0 else u)
             remote(
-                src.at[it, dest], dst.at[it, q], a2a_send.at[it, which], a2a_recv.at[it, which], {"py": dest}
+                src.at[it, dest],
+                dst.at[it, q],
+                a2a_send.at[it, which],
+                a2a_recv.at[it, which, own_group],
+                {"py": dest},
             ).start()
 
+    def await_group(dst, it, which, t):
+        g = lax.rem(own_group + G - t, G)
+        await_bytes(dst.at[it, pl.ds(0, 4 if t else 3)], a2a_recv.at[it, which, g])
+        return g
+
+    groups = [lax.rem(own_group + t, G) for t in far_groups]
+
+    def fetch_x(t):
+        c = lax.rem(p + PX - t, PX)
+        if t:
+            await_bytes(xrecv.at[0], a2a_recv.at[0, 0, c])
+        lhs[:, block(c, XL)] = xrecv[c]
+        return c
+
     def x_forward(it):
-        for t in list(range(1, G)) + [0]:
-            g = lax.rem(q // 4 + t, G)
-            tile = product(lhs, block(g, 256))
+        def turn(i, g, tile):
             turned = jnp.concatenate([tile[:, :128], tile[:, 128:]], axis=0).T
             ysend[it, block(g, 4)] = turned.astype(BF16).reshape(4, 32, 128)
-            scatter_tile(ysend, yrecv, it, 1, t, g)
+            scatter_tile(ysend, yrecv, it, 1, far_groups[i], g)
+
+        if it == 0:
+            count = iter(range(G))
+            in_steps([0] + far, XL, fetch_x, lambda g, tile: turn(next(count), g, tile), groups)
+        else:
+            for i, g in enumerate(groups):
+                turn(i, g, product(lhs, slice(None), block(g, 256)))
         sent_later(ysend.at[it, pl.ds(0, PY - 1)], a2a_send.at[it, 1])
 
-    def y_arrive(it):
-        await_bytes(yrecv.at[it, pl.ds(0, PY - 1)], a2a_recv.at[it, 1])
-        for m in range(PY // 2):
-            even, odd = yrecv[it, 2 * m].astype(F32), yrecv[it, 2 * m + 1].astype(F32)
-            low = jnp.where(half_lane, even, pltpu.roll(odd, 64, 1))
-            high = jnp.where(half_lane, pltpu.roll(even, 64, 1), odd)
-            lhs[0:32, m * 128 : (m + 1) * 128] = low.astype(BF16)
-            lhs[32:64, m * 128 : (m + 1) * 128] = high.astype(BF16)
+    def fetch_y(it):
+        def fetch(t):
+            g = await_group(yrecv, it, 1, t)
+            for m in range(2):
+                even = yrecv[it, 4 * g + 2 * m].astype(F32)
+                odd = yrecv[it, 4 * g + 2 * m + 1].astype(F32)
+                low = jnp.where(half_lane, even, pltpu.roll(odd, 64, 1))
+                high = jnp.where(half_lane, pltpu.roll(even, 64, 1), odd)
+                cols = block(2 * g + m, 128)
+                lhs[0:32, cols] = low.astype(BF16)
+                lhs[32:64, cols] = high.astype(BF16)
+            return g
+
+        return fetch
 
     def spectral(it, alpha):
-        acc = jnp.zeros((8, 128), F32)
-        for t in range(G):
-            cols = slice(t * 256, (t + 1) * 256)
-            tile = product(lhs, cols)
+        sums = []
+
+        def scale(n, tile):
+            cols = block(n, 256)
             if it == 0:
                 s2[:, cols] = tile
             else:
-                tile = s2[:, cols] - alpha * tile
+                tile = s2[:, cols] - alpha() * tile
             scaled = (tile * dinv[:, cols]).astype(BF16)
             s3[:, cols] = scaled
-            acc = acc + fold(tile * scaled.astype(F32))
-        return acc
+            sums.append(fold(tile * scaled.astype(F32)))
+
+        in_steps(far_groups, 256, fetch_y(it), scale, range(G))
+        return sum(sums[1:], sums[0])
 
     def y_back(it):
-        for t in list(range(1, G)) + [0]:
-            g = lax.rem(q // 4 + t, G)
-            tile = product(s3, block(g, 256))
+        for i, g in enumerate(groups):
+            tile = product(s3, slice(None), block(g, 256))
             for h in range(2):
                 low, high = tile[0:32, h * 128 : h * 128 + 128], tile[32:64, h * 128 : h * 128 + 128]
                 even = jnp.where(half_lane, low, pltpu.roll(high, 64, 1))
                 odd = jnp.where(half_lane, pltpu.roll(low, 64, 1), high)
                 zsend[it, g * 4 + 2 * h] = even.astype(BF16)
                 zsend[it, g * 4 + 2 * h + 1] = odd.astype(BF16)
-            scatter_tile(zsend, zrecv, it, 2, t, g)
+            scatter_tile(zsend, zrecv, it, 2, far_groups[i], g)
         sent_later(zsend.at[it, pl.ds(0, PY - 1)], a2a_send.at[it, 2])
 
-    def z_arrive(it):
-        await_bytes(zrecv.at[it, pl.ds(0, PY - 1)], a2a_recv.at[it, 2])
-        for g in range(G):
-            turned = zrecv[it, 4 * g : 4 * g + 4].reshape(128, 128).astype(F32).T.astype(BF16)
-            lhs[:, g * 256 : g * 256 + 128] = turned[0:64]
-            lhs[:, g * 256 + 128 : g * 256 + 256] = turned[64:128]
+    def fetch_z(it):
+        def fetch(t):
+            g = await_group(zrecv, it, 2, t)
+            turned = zrecv[it, block(g, 4)].reshape(128, 128).astype(F32).T.astype(BF16)
+            lhs[:, block(2 * g, 128)] = turned[0:64]
+            lhs[:, block(2 * g + 1, 128)] = turned[64:128]
+            return g
+
+        return fetch
 
     def line_copies(h):
         return [
@@ -428,16 +484,17 @@
         ]
 
     def x_back(it):
-        for c in range(PX):
-            tile = product(lhs, slice(c * XL, (c + 1) * XL)).astype(BF16)
-            bsend[it, c] = tile
-            zp[it, TOP:END, c * XL : (c + 1) * XL] = tile.astype(F32)
-            remote(
-                bsend.at[it, c], above.at[it, c], line_send.at[it, 2], line_recv.at[it, 2], west_of
-            ).start()
-            remote(
-                bsend.at[it, c], below.at[it, c], line_send.at[it, 3], line_recv.at[it, 3], east_of
-            ).start()
+        def spread(n, tile):
+            for c in range(n * 256 // XL, (n + 1) * 256 // XL):
+                part = tile[:, c * XL - n * 256 : (c + 1) * XL - n * 256].astype(BF16)
+                bsend[it, c] = part
+                zp[it, TOP:END, c * XL : (c + 1) * XL] = part.astype(F32)
+                for dst, i, where in ((above, 2, west_of), (below, 3, east_of)):
+                    remote(
+                        bsend.at[it, c], dst.at[it, c], line_send.at[it, i], line_recv.at[it, i], where
+                    ).start()
+
+        in_steps(far_groups, 256, fetch_z(it), spread, range(G))
         row_send[it, 0] = zp[it, TOP : TOP + 1, :]
         row_send[it, 1] = zp[it, END - 1 : END, :]
         rows = start(line_copies(it))
@@ -461,7 +518,7 @@
             hrow_send[it, c, 0] = zp[it, TOP - 1 : TOP, cols]
             hrow_send[it, c, 1] = zp[it, END : END + 1, cols]
         trio = (
-            (bsend, brecv, a2a_send.at[it, 3], a2a_recv.at[it, 3]),
+            (bsend, brecv, a2a_send.at[it, 3], a2a_recv.at[it, 3, 0]),
             (hrow_send, hrow_recv, grid_send.at[it, 0], grid_recv.at[it, 0]),
             (edge_send, edge_recv, grid_send.at[it, 1], grid_recv.at[it, 1]),
         )
@@ -475,7 +532,7 @@
 
     def grid_arrive(it):
         for dst, recv in (
-            (brecv, a2a_recv.at[it, 3]),
+            (brecv, a2a_recv.at[it, 3, 0]),
             (hrow_recv, grid_recv.at[it, 0]),
             (edge_recv, grid_recv.at[it, 1]),
         ):
@@ -486,6 +543,15 @@
             remote(cls_recv.at[1], cls_recv.at[2], cls_sem.at[0, 2], cls_sem.at[1, 2], west_of),
             remote(cls_recv.at[1], cls_recv.at[0], cls_sem.at[0, 0], cls_sem.at[1, 0], east_of),
         ]
+
+    def send_classes():
+        for t in far:
+            k = lax.rem(p + t, PX)
+            remote(
+                cls_send.at[k], cls_recv.at[1, p], cls_sem.at[0, 1], cls_sem.at[1, 1], {"px": k}
+            ).start()
+        cls_recv[1, p] = cls_send[p]
+        sent_later(cls_recv.at[1, pl.ds(0, PX - 1)], cls_sem.at[0, 1])
 
     def pencil_coefficients():
         await_bytes(cls_recv.at[1, pl.ds(0, PX - 1)], cls_sem.at[1, 1])
@@ -534,35 +600,31 @@
         wait_all(rows)
         zp[it, TOP - 1 : TOP, :] = row_recv[it, 0] * has_north
         zp[it, END : END + 1, :] = row_recv[it, 1] * has_south
-        await_bytes(above.at[it], line_recv.at[it, 2])
-        await_bytes(below.at[it], line_recv.at[it, 3])
-        to_grid(it)
-        if it == 1:
-            for r in range(0, ROWS + 16, 16):
-                if r == 0:
-                    at = slice(TOP - 1, 16)
-                elif r == ROWS:
-                    at = slice(ROWS, END + 1)
-                else:
-                    at = slice(r, r + 16)
-                zp[1, at, :] = zp[1, at, :] + beta * zp[0, at, :]
-        acc = jnp.zeros((8, 128), F32)
         for r in range(0, ROWS, 16):
             at = slice(r, r + 16)
             here = zp[it, TOP + r : TOP + r + 16, :]
-            up, down = beside(above, it, r), beside(below, it, r)
-            if it == 1:
-                up = up + beta * beside(above, 0, r)
-                down = down + beta * beside(below, 0, r)
             out = p_sum[at, :] * here - p_e[at, :] * pltpu.roll(here, N - 1, 1)
             out = out - p_w[at, :] * pltpu.roll(here, 1, 1)
             out = out - p_n[at, :] * zp[it, TOP - 1 + r : TOP + 15 + r, :]
-            out = out - p_s[at, :] * zp[it, TOP + 1 + r : TOP + 17 + r, :]
-            out = out - p_u[at, :] * up - p_d[at, :] * down
+            inner[at, :] = out - p_s[at, :] * zp[it, TOP + 1 + r : TOP + 17 + r, :]
+        ratio = None if beta is None else beta()
+        await_bytes(above.at[it], line_recv.at[it, 2])
+        await_bytes(below.at[it], line_recv.at[it, 3])
+        if it == 1:
+            to_grid(it)
+        sums = jnp.zeros((8, 128), F32)
+        for r in range(0, ROWS, 16):
+            at = slice(r, r + 16)
+            here = zp[it, TOP + r : TOP + r + 16, :]
+            out = inner[at, :] - p_u[at, :] * beside(above, it, r) - p_d[at, :] * beside(below, it, r)
             if it == 0:
+                image_0[at, :] = out
                 lhs[at, :] = out.astype(BF16)
-            acc = acc + fold(here * out)
-        return acc
+            else:
+                here = here + ratio * zp[0, TOP + r : TOP + r + 16, :]
+                out = out + ratio * image_0[at, :]
+            sums = sums + fold(here * out)
+        return sums
 
     def reduce_start(a, first, second_part):
         mine = jnp.concatenate(
@@ -631,50 +693,52 @@
                 direction[k] = value
             vp[k, TOP:END, :] = value
 
-    await_bytes(xrecv.at[pl.ds(0, PX - 1)], a2a_recv.at[0, 0])
-    for c in range(PX):
-        lhs[:, c * XL : (c + 1) * XL] = xrecv[c]
     x_forward(0)
-    coeff_rows = pencil_coefficients()
-    y_arrive(0)
+    send_classes()
     gamma_part = spectral(0, None)
     y_back(0)
+    coeff_rows = pencil_coefficients()
+    rows = x_back(0)
     pencil_weights(coeff_rows)
-    z_arrive(0)
-    rows = x_back(0)
     curve = pencil_operator(0, rows, None)
     reduce_start(0, gamma_part, curve)
 
     x_forward(1)
     reduce_middle(0)
+    to_grid(0)
+    known = []
+
+    def first_alpha():
+        if not known:
+            gamma, curve = reduce_end(0)
+            known.extend([gamma, gamma / curve])
+        return known[1]
+
+    reduce_start(1, spectral(1, first_alpha), zero)
+    gamma0, alpha0 = known
+    y_back(1)
     grid_arrive(0)
+    reduce_middle(1)
     grid_direction(0, vp_0, None)
 
     @pl.loop(0, NZ)
     def _(k):
-        image[k] = operator(vp_0, k)
-
-    y_arrive(1)
-    gamma0, curve0 = reduce_end(0)
-    alpha0 = gamma0 / curve0
-    reduce_start(1, spectral(1, alpha0), zero)
-    y_back(1)
-
-    @pl.loop(0, NZ)
-    def _(k):
-        res[k] = res[k] - alpha0 * image[k]
+        res[k] = res[k] - alpha0 * operator(vp_0, k)
         sol[k] = vp_x[k, TOP:END, :] + alpha0 * vp_0[k, TOP:END, :]
 
     store_x = pltpu.make_async_copy(sol, sol_hbm, store_sem.at[0])
     store_r = pltpu.make_async_copy(res, res_hbm, store_sem.at[1])
     store_x.start()
     store_r.start()
-    reduce_middle(1)
-    z_arrive(1)
     rows = x_back(1)
-    gamma1, _ = reduce_end(1)
-    beta = gamma1 / gamma0
-    reduce_start(2, pencil_operator(1, rows, beta), zero)
+
+    def second_ratio():
+        gamma, _ = reduce_end(1)
+        known.extend([gamma, gamma / gamma0])
+        return known[3]
+
+    reduce_start(2, pencil_operator(1, rows, second_ratio), zero)
+    gamma1, beta = known[2:]
 
     reduce_middle(2)
     grid_arrive(1)
@@ -702,11 +766,29 @@
     store_a.wait()
 
 
-def last_update(alpha, x, r, d, image, sol, res, direction):
-    step = alpha[0:1, 0:1]
-    sol[...] = x[...] + step * d[...]
-    res[...] = r[...] - step * image[...]
-    direction[...] = d[...]
+def last_update(alpha, x, r, d, image, sol, res, direction, av, xv, rv, dv, iv, load, store):
+    loads = [
+        pltpu.make_async_copy(src, dst, load.at[i])
+        for i, (src, dst) in enumerate(((alpha, av), (d, dv), (x, xv), (image, iv), (r, rv)))
+    ]
+    for copy in loads:
+        copy.start()
+    for copy in loads[:2]:
+        copy.wait()
+    stores = [pltpu.make_async_copy(dv, direction, store.at[0])]
+    stores[0].start()
+    step = av[0:1, 0:1]
+    loads[2].wait()
+    xv[...] = xv[...] + step * dv[...]
+    stores.append(pltpu.make_async_copy(xv, sol, store.at[1]))
+    stores[1].start()
+    loads[3].wait()
+    loads[4].wait()
+    rv[...] = rv[...] - step * iv[...]
+    stores.append(pltpu.make_async_copy(rv, res, store.at[2]))
+    stores[2].start()
+    for copy in stores:
+        copy.wait()
 
 
 def shards(PX, PY, right_side, solution_in, classes, coeff_table, eigenvectors, eigenvalues, level_shift):
@@ -732,14 +814,17 @@
         eigenvalues.reshape(1, N),
         level_shift,
     )
-    levels = pl.BlockSpec((2, ROWS, XL), lambda k: (k, 0, 0))
+    field = pltpu.VMEM(out.shape, F32)
     return tuple(
         pl.pallas_call(
             last_update,
-            grid=(PX // 2,),
             out_shape=[out] * 3,
-            in_specs=[pl.BlockSpec((1, 128), lambda k: (0, 0))] + [levels] * 4,
-            out_specs=[levels] * 3,
+            in_specs=[hbm] * 5,
+            out_specs=[hbm] * 3,
+            scratch_shapes=[pltpu.VMEM((1, 128), F32)]
+            + [field] * 4
+            + [pltpu.SemaphoreType.DMA((5,)), pltpu.SemaphoreType.DMA((3,))],
+            compiler_params=pltpu.CompilerParams(vmem_limit_bytes=60 * 2**20),
         )(alpha, x, r, d, image)
     )
 

time: 97 us -> 93.2 us (0.961)
  Pallas kernels: 96.2 us -> 92.3 us
    pallas_call x1, Pallas kernels: 92.4 us -> 89.9 us  [shards(): pl.pallas_call(functools.partial(kernel, PX, PY, tuple(buffers)), out_sha...]
    pallas_call x1, Pallas kernels: 3.84 us -> 2.44 us  [shards(): pl.pallas_call(last_update, out_shape=[out] * 3, in_specs=[hbm] * 5, out_...]
where the time goes in v4:
time: 93.2 us; the launch traced here: 93.1 us
  Pallas kernels  92.3 us (99%)
    pallas_call x1, Pallas kernels, shards(): pl.pallas_call(functools.partial(kernel, PX, PY, tuple(buffers)), out_sha...  89.9 us
    pallas_call x1, Pallas kernels, shards(): pl.pallas_call(last_update, out_shape=[out] * 3, in_specs=[hbm] * 5, out_...  2.44 us

profile of v4, /device:TPU:1, one launch (start us, length us, event | category | flops | bytes accessed | tf_op | source)
XLA Modules:
  0.0 93.1 jit_solution(10160518328808714691)
XLA Ops:
  0.6 89.9 %shard_map.94 = (f32[8,64,256]{2,1,0:T(8,128)}, f32[8,64,256]{2,1,0:T(8,128)}, f32[8,64,256]{2,1,0:T(8,128)}, f32[8,64,256]{2,1,0:T(8,128)}, f32[1,128]{1,0:T(1,128)}) custom-call(f32[8,64,256]{2,1,0:T(8,128)} %refs_0_.1, f32[8,64,256]{2,1,0:T(8,128)} %refs_1_.1, s32[8,64,256]{2,1,0:T(8,128)} %refs_2_.1, f32[16]{0:T(128)} %refs_3_.1, ...), custom_call_target="tpu_custom_call" | custom-call | tf_op jit(solution)/shard_map/pallas_call | solution.py:799
  90.5 2.4 %shard_map.95 = (f32[8,64,256]{2,1,0:T(8,128)}, f32[8,64,256]{2,1,0:T(8,128)}, f32[8,64,256]{2,1,0:T(8,128)}) custom-call(f32[1,128]{1,0:T(1,128)} %get-tuple-element.8.alpha, f32[8,64,256]{2,1,0:T(8,128)} %get-tuple-element.9.x, f32[8,64,256]{2,1,0:T(8,128)} %get-tuple-element.10.r, f32[8,64,256]{2,1,0:T(8,128)} %get-tuple-element.11.d, ...), custom_call_target="tpu_custom_call" | custom-call | tf_op jit(solution)/shard_map/pallas_call | solution.py:819

commit v5 on v4

--- a/solution.py
+++ b/solution.py
@@ -307,8 +307,7 @@
     def west(values, edge):
         return jnp.where(lanes == 0, edge, pltpu.roll(values, 1, 1))
 
-    @pl.loop(0, NZ)
-    def _(k):
+    def weights(k):
         here = cp[k, TOP:END, :]
         edge = chalo[k]
         to_e = 0.5 * (here + east(here, edge))
@@ -340,6 +339,7 @@
     load_b.wait()
     for t in far + [0]:
         k = lax.rem(p + t, NZ)
+        weights(k)
         value = res[k] - operator(vp_x, k)
         res[k] = value
         if t:
@@ -444,15 +444,24 @@
 
         def scale(n, tile):
             cols = block(n, 256)
-            if it == 0:
-                s2[:, cols] = tile
-            else:
-                tile = s2[:, cols] - alpha() * tile
             scaled = (tile * dinv[:, cols]).astype(BF16)
             s3[:, cols] = scaled
             sums.append(fold(tile * scaled.astype(F32)))
 
-        in_steps(far_groups, 256, fetch_y(it), scale, range(G))
+        def keep(n, tile):
+            cols = block(n, 256)
+            if it == 0:
+                s2[:, cols] = tile
+                scale(n, tile)
+            else:
+                acc[:, cols] = tile
+
+        in_steps(far_groups, 256, fetch_y(it), keep, range(G))
+        if it == 1:
+            step = alpha()
+            for n in range(G):
+                cols = block(n, 256)
+                scale(n, s2[:, cols] - step * acc[:, cols])
         return sum(sums[1:], sums[0])
 
     def y_back(it):
@@ -718,7 +727,6 @@
     gamma0, alpha0 = known
     y_back(1)
     grid_arrive(0)
-    reduce_middle(1)
     grid_direction(0, vp_0, None)
 
     @pl.loop(0, NZ)
@@ -730,6 +738,7 @@
     store_r = pltpu.make_async_copy(res, res_hbm, store_sem.at[1])
     store_x.start()
     store_r.start()
+    reduce_middle(1)
     rows = x_back(1)
 
     def second_ratio():

time: 93.2 us -> 92.3 us (level)
  no operation moved by 1% of the time
where the time goes in v5:
time: 92.3 us; the launch traced here: 92.2 us
  Pallas kernels  91.4 us (99%)
    pallas_call x1, Pallas kernels, shards(): pl.pallas_call(functools.partial(kernel, PX, PY, tuple(buffers)), out_sha...  89 us
    pallas_call x1, Pallas kernels, shards(): pl.pallas_call(last_update, out_shape=[out] * 3, in_specs=[hbm] * 5, out_...  2.44 us

profile of v5, /device:TPU:1, one launch (start us, length us, event | category | flops | bytes accessed | tf_op | source)
XLA Modules:
  0.0 92.2 jit_solution(18391570173833488659)
XLA Ops:
  0.6 89.0 %shard_map.94 = (f32[8,64,256]{2,1,0:T(8,128)}, f32[8,64,256]{2,1,0:T(8,128)}, f32[8,64,256]{2,1,0:T(8,128)}, f32[8,64,256]{2,1,0:T(8,128)}, f32[1,128]{1,0:T(1,128)}) custom-call(f32[8,64,256]{2,1,0:T(8,128)} %refs_0_.1, f32[8,64,256]{2,1,0:T(8,128)} %refs_1_.1, s32[8,64,256]{2,1,0:T(8,128)} %refs_2_.1, f32[16]{0:T(128)} %refs_3_.1, ...), custom_call_target="tpu_custom_call" | custom-call | tf_op jit(solution)/shard_map/pallas_call | solution.py:808
  89.6 2.4 %shard_map.95 = (f32[8,64,256]{2,1,0:T(8,128)}, f32[8,64,256]{2,1,0:T(8,128)}, f32[8,64,256]{2,1,0:T(8,128)}) custom-call(f32[1,128]{1,0:T(1,128)} %get-tuple-element.8.alpha, f32[8,64,256]{2,1,0:T(8,128)} %get-tuple-element.9.x, f32[8,64,256]{2,1,0:T(8,128)} %get-tuple-element.10.r, f32[8,64,256]{2,1,0:T(8,128)} %get-tuple-element.11.d, ...), custom_call_target="tpu_custom_call" | custom-call | tf_op jit(solution)/shard_map/pallas_call | solution.py:828
